TPU v7x, 256 devices: a whole 4x4x8 slice. The times are simulated.
256 devices in a mesh: region: 32 (over x, z), sub: 8 (over y, core).
Axes of the slice: x: 4, y: 4, z: 8, core: 2. Of those that a mesh axis runs over, the one named last changes fastest.
Arguments:
- directions: float32 [2, 64, 256, 2048], P(None, None, 'region', 'sub'), may hold values from -6 to 6
- diag_blocks: float32 [4, 4, 256, 2048], P(None, None, 'region', 'sub'), may hold values from -2 to 2
- left_blocks: float32 [4, 4, 256, 2048], P(None, None, 'region', 'sub'), may hold values from -1.5 to 1.5
- right_blocks: float32 [4, 4, 256, 2048], P(None, None, 'region', 'sub'), may hold values from -1.5 to 1.5
- param_blocks: float32 [4, 2, 256, 2048], P(None, None, 'region', 'sub'), may hold values from -6 to 6
- obs_weight: float32 [4, 256, 2048], P(None, 'region', 'sub'), may hold values from 0.3 to 3
- end_junction: int32 [2, 256, 1], replicated, may hold values from 0 to 255
Outputs:
- hess_dirs: float32 [2, 64, 256, 2048], P(None, None, 'region', 'sub')
Inputs may be any that keep to these rules, and one draw needn't show every extreme that they name: `end_junction`: every junction is named by at least one pipe end.
All inputs are finite; a program needn't handle non-finite values.
Results may differ from a plain program's by a relative error of at most 0.0001.
Values sent between devices are 32-bit elements; how exact they have to be, the bound alone decides.
A program may use at most 128 MiB of HBM per device.

v0:
```python
import jax
import jax.numpy as jnp
from jax import lax
from jax.sharding import PartitionSpec as P

JUNC_DEV = 1


junction_rate = 0.5


def padded_2(cells, sides, width):
    for axis, dim in sides:
        count = lax.axis_size(axis)
        ends = count - 1
        head = lax.slice_in_dim(cells, 0, width, axis=dim)
        tail = lax.slice_in_dim(cells, cells.shape[dim] - width, cells.shape[dim], axis=dim)
        cells = jnp.concatenate(
            [
                lax.ppermute(tail, axis, [(i, (i + 1) % count) for i in range(ends)]),
                cells,
                lax.ppermute(head, axis, [((i + 1) % count, i) for i in range(ends)]),
            ],
            axis=dim,
        )
    return cells


def passed_along(block, axis, distance):
    devices = range(lax.axis_size(axis))
    route = [(i - distance, i) for i in devices if i - distance in devices]
    return lax.ppermute(block, axis, route)


def block_apply(blocks, state_in, flipped):
    out_count = blocks.shape[1] if flipped else blocks.shape[0]
    summed = jnp.zeros((out_count,) + state_in.shape[1:], jnp.float32)
    for member in range(state_in.shape[0]):
        factor = blocks[member] if flipped else blocks[:, member]
        summed = summed + factor[:, None] * state_in[member][None]
    return summed


def neighbours(state_in):
    padded = padded_2(state_in, (("sub", 3),), 1)
    return (padded[..., :-2], padded[..., 2:])


def junction_add(state_in, onehot, degree, is_first):
    components, columns, pipe_count = (state_in.shape[0], state_in.shape[1], state_in.shape[2])
    edge_vals = jnp.where(is_first, state_in[..., 0], state_in[..., -1])
    end_states = jnp.transpose(edge_vals, (2, 0, 1)).reshape(pipe_count, components * columns)
    totals = lax.psum(
        jnp.dot(
            onehot.T,
            end_states,
            precision=lax.Precision.HIGHEST,
            preferred_element_type=jnp.float32,
        ),
        ("region", "sub"),
    )
    gathered = jnp.dot(
        onehot, totals, precision=lax.Precision.HIGHEST, preferred_element_type=jnp.float32
    )
    means = gathered / degree[:, None]
    added = junction_rate * (means - end_states)
    return jnp.transpose(added.reshape(pipe_count, components, columns), (1, 2, 0))


def on_device(
    directions, diag_blocks, left_blocks, right_blocks, param_blocks, obs_weight, end_junction
):
    region_count = lax.axis_size("region")
    sub_count = lax.axis_size("sub")
    sub_index = lax.axis_index("sub")
    is_first = sub_index == 0
    is_last = sub_index == sub_count - 1
    active = jnp.logical_or(is_first, is_last)
    pipe_count = directions.shape[2]
    junctions = JUNC_DEV * region_count * sub_count
    all_ids = end_junction[:, :, 0]
    first_pipe = lax.axis_index("region") * pipe_count
    upstream_ids = lax.dynamic_slice_in_dim(all_ids[0], first_pipe, pipe_count, 0)
    downstream_ids = lax.dynamic_slice_in_dim(all_ids[1], first_pipe, pipe_count, 0)
    my_ids = jnp.where(is_first, upstream_ids, downstream_ids)
    degree = jnp.sum((all_ids.reshape(-1)[None, :] == my_ids[:, None]).astype(jnp.float32), axis=1)
    junction_range = jnp.arange(junctions, dtype=jnp.int32)
    onehot = (my_ids[:, None] == junction_range[None, :]).astype(jnp.float32) * active.astype(
        jnp.float32
    )
    next_left = passed_along(left_blocks[..., :1], "sub", -1)
    prev_right = passed_along(right_blocks[..., -1:], "sub", 1)
    left_next = jnp.concatenate([left_blocks[..., 1:], next_left], axis=3)
    right_prev = jnp.concatenate([prev_right, right_blocks[..., :-1]], axis=3)

    def with_junctions(result, state_in):
        added = junction_add(state_in, onehot, degree, is_first)
        result = result.at[..., 0].add(jnp.where(is_first, added, 0.0))
        return result.at[..., -1].add(jnp.where(is_last, added, 0.0))

    source = block_apply(param_blocks, directions, False)
    state = source
    upstream, downstream = neighbours(state)
    result = block_apply(diag_blocks, state, False)
    result = result + block_apply(left_blocks, upstream, False)
    result = result + block_apply(right_blocks, downstream, False)
    state = with_junctions(result, state) + source
    adjoint = obs_weight[:, None] * state
    hess = block_apply(param_blocks, adjoint, True)
    upstream, downstream = neighbours(adjoint)
    result = block_apply(diag_blocks, adjoint, True)
    result = result + block_apply(left_next, downstream, True)
    result = result + block_apply(right_prev, upstream, True)
    adjoint = with_junctions(result, adjoint)
    hess = hess + block_apply(param_blocks, adjoint, True)
    return hess


def solution(mesh):
    return jax.shard_map(
        on_device,
        mesh=mesh,
        in_specs=(
            P(None, None, "region", "sub"),
            P(None, None, "region", "sub"),
            P(None, None, "region", "sub"),
            P(None, None, "region", "sub"),
            P(None, None, "region", "sub"),
            P(None, "region", "sub"),
            P(),
        ),
        out_specs=P(None, None, "region", "sub"),
        check_vma=False,
    )
```

profile of v0, /device:TPU:32, one launch (start us, length us, event | category | flops | bytes accessed | tf_op | source)
XLA Modules:
  0.0 576.1 jit_solution(12747576173339316089)
XLA Ops:
  10.6 6.0 %multiply_add_fusion = f32[4,64,8,256]{1,0,2,3:T(4,128)S(1)} fusion(f32[64,8,256]{0,1,2:T(8,128)S(1)} %copy.50, f32[4,8,256]{0,1,2:T(8,128)} %copy.49, f32[64,8,256]{0,1,2:T(8,128)S(1)} %copy.48, f32[4,8,256]{0,1,2:T(8,128)S(1)} %copy.47), kind=kLoop, calls=%fused_computation.3 | loop fusion | flops 1572864 | bytes 3211264 | tf_op jit(solution)/shard_map/add | solution.py:40
  16.6 1.9 copy-done
  20.4 3.6 collective-permute-start
  30.1 3.8 collective-permute-start.4
  37.3 1.4 slice_bitcast_fusion.23
  38.7 2.1 copy.46
  40.8 2.1 copy.51
  42.9 2.1 copy.52
  45.0 2.2 copy.53
  49.9 1.4 copy.56
  54.0 2.1 copy.59
  56.1 1.4 copy.60
  59.6 2.1 copy.45
  61.7 2.1 copy.66
  63.8 2.1 copy.67
  67.3 1.4 copy.69
  75.9 1.4 copy.74
  81.3 26.3 %pad_maximum_fusion.11 = (f32[1,64,8,256]{1,0,2,3:T(1,128)}, f32[1,64,8,256]{1,0,2,3:T(1,128)}, f32[1,64,8,256]{1,0,2,3:T(1,128)}, f32[1,64,8,256]{1,0,2,3:T(1,1...) fusion(f32[4,64,8,1]{1,0,2,3:T(4,128)} %collective-permute-done, ...), kind=kLoop, calls=%fused_computation.21 | loop fusion | flops 524288 | bytes 12599296 | tf_op jit(solution)/shard_map/slice | solution.py:40
  107.6 5.4 pad_maximum_fusion.15
  113.0 30.5 %add_add_fusion.1 = f32[4,64,8,256]{1,0,2,3:T(4,128)} fusion(f32[64,8,256]{0,1,2:T(8,128)} %bitcast.135, f32[4,8,256]{0,1,2:T(8,128)} %copy.61, f32[64,8,256]{0,1,2:T(8,128)} %bitcast.133, f32[4,8,256]{0,1,2:T(8,128)} %copy.60, f32[64,8,256]{0,1,2:T(8,128)} %bitcast.134, f32[4,8,256]{0,1,2:T(8,128)} %copy.59, f32[64,8,256]{0,1,2:T(8,128)} %bitcast.132, ...), kind=kLoop, calls=%fused_computation.2 | loop fusion | flops 12058624 | bytes 8781824 | tf_op jit(solution)/shard_map/add | solution.py:106
  143.6 134.7 %all-reduce.3.cloned.1.call-done = f32[256,256]{1,0:T(8,128)} async-done(((f32[256,256]{1,0:T(8,128)}), f32[256,256]{1,0:T(8,128)}) %all-reduce.3.cloned.1.call-update) | async-done | bytes 262160 | tf_op jit(solution)/shard_map/psum | solution.py:53
  282.3 9.2 %add_multiply_fusion = f32[4,64,8,256]{1,0,2,3:T(4,128)S(1)} fusion(f32[4,64,8,256]{1,0,2,3:T(4,128)} %fusion.20, f32[4,8,256]{0,1,2:T(8,128)} %copy.45, f32[64,8,256]{0,1,2:T(8,128)S(1)} %copy.50, f32[4,8,256]{0,1,2:T(8,128)} %copy.49, f32[64,8,256]{0,1,2:T(8,128)S(1)} %copy.48, f32[4,8,256]{0,1,2:T(8,128)S(1)} %copy.47), kind=kLoop, calls=%fused_computation.1 | loop fusion | flops 2621440 | bytes 5341184 | tf_op jit(solution)/shard_map/mul | solution.py:108
  291.5 1.9 copy-done.2
  296.1 3.4 collective-permute-start.5
  299.5 11.5 %pad_maximum_fusion.7 = (f32[1,64,8,256]{1,0,2,3:T(1,128)}, f32[1,64,8,256]{1,0,2,3:T(1,128)}, f32[1,64,8,256]{1,0,2,3:T(1,128)}, f32[1,64,8,256]{1,0,2,3:T(1,128)}) fusion(f32[4,64,8,1]{1,0,2,3:T(4,128)S(1)} %collective-permute-done.3, f32[4,64,8,256]{1,0,2,3:T(4,128)} %copy-done.2), kind=kLoop, calls=%fused_computation.17 | loop fusion | flops 524288 | bytes 4202496 | tf_op jit(solution)/shard_map/slice | solution.py:40
  311.0 7.4 %pad_maximum_fusion.3 = (f32[1,64,8,256]{1,0,2,3:T(1,128)}, f32[1,64,8,256]{1,0,2,3:T(1,128)}, f32[1,64,8,256]{1,0,2,3:T(1,128)}, f32[1,64,8,256]{1,0,2,3:T(1,12...) fusion(f32[4,64,8,256]{1,0,2,3:T(4,128)S(1)} %copy-done.3, ...), kind=kLoop, calls=%fused_computation.13 | loop fusion | flops 524288 | bytes 12599296 | tf_op jit(solution)/shard_map/slice | solution.py:40
  318.4 30.3 %add_add_fusion = f32[4,64,8,256]{1,0,2,3:T(4,128)} fusion(f32[64,8,256]{0,1,2:T(8,128)} %bitcast.143, f32[4,8,256]{0,1,2:T(8,128)} %copy.77, f32[64,8,256]{0,1,2:T(8,128)} %bitcast.142, f32[4,8,256]{0,1,2:T(8,128)} %copy.76, f32[64,8,256]{0,1,2:T(8,128)} %bitcast.141, f32[4,8,256]{0,1,2:T(8,128)} %copy.75, f32[64,8,256]{0,1,2:T(8,128)} %bitcast.140, ...), kind=kLoop, calls=%fused_computation | loop fusion | flops 12058624 | bytes 8781824 | tf_op jit(solution)/shard_map/add | solution.py:113
  348.7 2.4 copy.62
  354.7 191.3 %all-reduce.5.cloned.1.call-done = f32[256,256]{1,0:T(8,128)} async-done(((f32[256,256]{1,0:T(8,128)}), f32[256,256]{1,0:T(8,128)}) %all-reduce.5.cloned.1.call-update) | async-done | bytes 262160 | tf_op jit(solution)/shard_map/psum | solution.py:53
  550.0 11.3 %fusion.45 = (f32[1,64,8,256]{1,0,2,3:T(1,128)}, f32[1,64,8,256]{1,0,2,3:T(1,128)S(1)}, f32[1,64,8,256]{1,0,2,3:T(1,128)S(1)}, f32[1,64,8,256]{1,0,2,3:T(1,128)S(1)}) fusion(f32[4,64,8,256]{1,0,2,3:T(4,128)} %fusion.18), kind=kLoop, calls=%fused_computation.121 | loop fusion | bytes 4194304 | tf_op jit(solution)/shard_map/slice | solution.py:40
  561.3 2.5 copy.78
  565.9 3.3 add_add_fusion.2
  (112 shorter events, 51.7 us)
Async XLA Ops:
  6.5 2.3 copy-start.8
  6.5 271.8 %all-reduce.3.cloned.1.call-start = ((), (), s32[]{:S(2)}) async-start(), calls=%async_computation | async-start | bytes 524288 | tf_op jit(solution)/shard_map/psum | solution.py:53
  10.6 13.5 %copy-start.22 = (s32[2,256,1]{1,2,0:T(1,128)S(1)}, s32[2,256,1]{1,2,0:T(1,128)}, u32[]{:S(2)}) copy-start(s32[2,256,1]{1,2,0:T(1,128)} %param.21) | copy-start | bytes 6148
  10.6 16.8 %copy-start.4 = (f32[4,4,8,256]{3,2,1,0:T(8,128)S(1)}, f32[4,4,8,256]{3,2,1,0:T(8,128)}, u32[]{:S(2)}) copy-start(f32[4,4,8,256]{3,2,1,0:T(8,128)} %param.17) | copy-start | bytes 393220
  10.6 18.8 %copy-start.5 = (f32[4,4,8,256]{3,2,1,0:T(8,128)S(1)}, f32[4,4,8,256]{3,2,1,0:T(8,128)}, u32[]{:S(2)}) copy-start(f32[4,4,8,256]{3,2,1,0:T(8,128)} %param.18) | copy-start | bytes 393220
  10.6 25.4 %copy-start.6 = (f32[4,4,8,256]{3,2,1,0:T(8,128)S(1)}, f32[4,4,8,256]{3,2,1,0:T(8,128)}, u32[]{:S(2)}) copy-start(f32[4,4,8,256]{3,2,1,0:T(8,128)} %param.16) | copy-start | bytes 393220
  16.6 2.0 copy-start
  19.2 62.1 %collective-permute-start.1 = (f32[4,64,8,1]{1,0,2,3:T(4,128)}, f32[4,64,8,1]{1,0,2,3:T(4,128)}, u32[]{:S(2)}, u32[]{:S(2)}) collective-permute-start(f32[4,64,8,1]{1,0,2,3:T(4,128)} %get-tuple-element.81), channel_id=1, source_target_pairs={{1,0},{2,1},{3,2},{4,3},{5,4},{6,5},{7,6},{9,8},{10,9},{11,10},{12... | collective-permute-start | bytes 24584 | tf_op jit(solution)/shard_map/ppermute | solution.py:22
  20.4 87.2 %collective-permute-start = (f32[4,64,8,1]{1,0,2,3:T(4,128)}, f32[4,64,8,1]{1,0,2,3:T(4,128)}, u32[]{:S(2)}, u32[]{:S(2)}) collective-permute-start(f32[4,64,8,1]{1,0,2,3:T(4,128)} %get-tuple-element.82), channel_id=1, source_target_pairs={{0,1},{1,2},{2,3},{3,4},{4,5},{5,6},{6,7},{8,9},{9,10},{10,11},{11... | collective-permute-start | bytes 24584 | tf_op jit(solution)/shard_map/ppermute | solution.py:20
  27.4 518.6 %all-reduce.5.cloned.1.call-start = ((), (), s32[]{:S(2)}) async-start(), calls=%async_computation.1 | async-start | bytes 524288 | tf_op jit(solution)/shard_map/psum | solution.py:53
  28.1 40.7 %collective-permute-start.2 = (f32[4,4,8,1]{3,2,1,0:T(8,128)}, f32[4,4,8,1]{3,2,1,0:T(8,128)}, u32[]{:S(2)}, u32[]{:S(2)}) collective-permute-start(f32[4,4,8,1]{3,2,1,0:T(8,128)} %slice.403), channel_id=1, source_target_pairs={{1,0},{2,1},{3,2},{4,3},{5,4},{6,5},{7,6},{9,8},{10,9},{11,10},{12... | collective-permute-start | bytes 1544 | tf_op jit(solution)/shard_map/ppermute | solution.py:32
  30.1 39.5 %collective-permute-start.4 = (f32[4,4,8,1]{3,2,1,0:T(8,128)}, f32[4,4,8,1]{3,2,1,0:T(8,128)}, u32[]{:S(2)}, u32[]{:S(2)}) collective-permute-start(f32[4,4,8,1]{3,2,1,0:T(8,128)} %slice.413), channel_id=1, source_target_pairs={{0,1},{1,2},{2,3},{3,4},{4,5},{5,6},{6,7},{8,9},{9,10},{10,11},{11... | collective-permute-start | bytes 1544 | tf_op jit(solution)/shard_map/ppermute | solution.py:32
  36.0 12.6 %copy-start.16 = (f32[4,8,256]{2,1,0:T(8,128)S(1)}, f32[4,8,256]{2,1,0:T(8,128)}, u32[]{:S(2)}) copy-start(f32[4,8,256]{2,1,0:T(8,128)} %get-tuple-element.108) | copy-start | bytes 98308
  36.0 13.9 %copy-start.15 = (f32[4,8,256]{2,1,0:T(8,128)S(1)}, f32[4,8,256]{2,1,0:T(8,128)}, u32[]{:S(2)}) copy-start(f32[4,8,256]{2,1,0:T(8,128)} %get-tuple-element.107) | copy-start | bytes 98308
  36.0 15.3 %copy-start.14 = (f32[4,8,256]{2,1,0:T(8,128)S(1)}, f32[4,8,256]{2,1,0:T(8,128)}, u32[]{:S(2)}) copy-start(f32[4,8,256]{2,1,0:T(8,128)} %get-tuple-element.106) | copy-start | bytes 98308
  37.3 9.9 %copy-start.17 = (f32[4,8,256]{2,1,0:T(8,128)S(1)}, f32[4,8,256]{2,1,0:T(8,128)}, u32[]{:S(2)}) copy-start(f32[4,8,256]{2,1,0:T(8,128)} %get-tuple-element.105) | copy-start | bytes 98308
  38.7 13.9 %copy-start.13 = (f32[4,8,256]{2,1,0:T(8,128)S(1)}, f32[4,8,256]{2,1,0:T(8,128)}, u32[]{:S(2)}) copy-start(f32[4,8,256]{2,1,0:T(8,128)} %get-tuple-element.109) | copy-start | bytes 98308
  42.9 13.2 %copy-start.11 = (f32[4,8,256]{2,1,0:T(8,128)S(1)}, f32[4,8,256]{2,1,0:T(8,128)}, u32[]{:S(2)}) copy-start(f32[4,8,256]{2,1,0:T(8,128)} %get-tuple-element.111) | copy-start | bytes 98308
  45.0 12.5 %copy-start.9 = (f32[4,8,256]{2,1,0:T(8,128)S(1)}, f32[4,8,256]{2,1,0:T(8,128)}, u32[]{:S(2)}) copy-start(f32[4,8,256]{2,1,0:T(8,128)} %get-tuple-element.110) | copy-start | bytes 98308
  51.3 14.6 %copy-start.12 = (f32[4,8,256]{2,1,0:T(8,128)S(1)}, f32[4,8,256]{2,1,0:T(8,128)}, u32[]{:S(2)}) copy-start(f32[4,8,256]{2,1,0:T(8,128)} %get-tuple-element.100) | copy-start | bytes 98308
  52.7 14.6 %copy-start.10 = (f32[4,8,256]{2,1,0:T(8,128)S(1)}, f32[4,8,256]{2,1,0:T(8,128)}, u32[]{:S(2)}) copy-start(f32[4,8,256]{2,1,0:T(8,128)} %get-tuple-element.99) | copy-start | bytes 98308
  54.0 14.7 %copy-start.7 = (f32[4,4,8,255]{3,2,1,0:T(8,128)S(1)}, f32[4,4,8,255]{3,2,1,0:T(8,128)}, u32[]{:S(2)}) copy-start(f32[4,4,8,255]{3,2,1,0:T(8,128)} %slice.402) | copy-start | bytes 391684
  81.3 26.3 %copy-start.1 = (f32[4,64,8,256]{1,0,2,3:T(4,128)S(1)}, f32[4,64,8,256]{1,0,2,3:T(4,128)}, u32[]{:S(2)}) copy-start(f32[4,64,8,256]{1,0,2,3:T(4,128)} %copy-done) | copy-start | bytes 6291460
  113.0 165.3 %copy-start.23 = (f32[8]{0:T(128)S(1)}, f32[8]{0:T(128)}, u32[]{:S(2)}) copy-start(f32[8]{0:T(128)} %convert_reduce_fusion) | copy-start | bytes 100
  291.5 2.0 copy-start.2
  293.6 5.9 %collective-permute-start.3 = (f32[4,64,8,1]{1,0,2,3:T(4,128)S(1)}, f32[4,64,8,1]{1,0,2,3:T(4,128)S(1)}, u32[]{:S(2)}, u32[]{:S(2)}) collective-permute-start(f32[4,64,8,1]{1,0,2,3:T(4,128)S(1)} %get-tuple-element.75), channel_id=1, source_target_pairs={{1,0},{2,1},{3,2},{4,3},{5,4},{6,5},{7,6},{9,8},{10,9},{11,10},{12... | collective-permute-start | bytes 24584 | tf_op jit(solution)/shard_map/ppermute | solution.py:22
  296.1 14.9 %copy-start.3 = (f32[4,64,8,256]{1,0,2,3:T(4,128)S(1)}, f32[4,64,8,256]{1,0,2,3:T(4,128)}, u32[]{:S(2)}) copy-start(f32[4,64,8,256]{1,0,2,3:T(4,128)} %copy-done.2) | copy-start | bytes 6291460
  296.1 14.9 %collective-permute-start.5 = (f32[4,64,8,1]{1,0,2,3:T(4,128)S(1)}, f32[4,64,8,1]{1,0,2,3:T(4,128)S(1)}, u32[]{:S(2)}, u32[]{:S(2)}) collective-permute-start(f32[4,64,8,1]{1,0,2,3:T(4,128)S(1)} %get-tuple-element.74), channel_id=1, source_target_pairs={{0,1},{1,2},{2,3},{3,4},{4,5},{5,6},{6,7},{8,9},{9,10},{10,11},{11... | collective-permute-start | bytes 24584 | tf_op jit(solution)/shard_map/ppermute | solution.py:20
  561.3 4.6 copy-start.18
  561.3 4.6 copy-start.19
  561.3 4.6 copy-start.20
  561.3 4.6 copy-start.21
Sparse Core Ops, SparseCore 0:
  27.5 250.7 all-reduce.2
  296.2 249.7 all-reduce.4
where the time goes:
time: 580 us; the launch traced here: 576 us
  waiting for transfers between devices  326 us (56%)
  other arithmetic  139 us (24%)
  local copies, waits for them, and re-layouts  77.9 us (13%)
  starting transfers between devices  14.7 us (3%)
  between operations  13.7 us (2%)
    psum x2, waiting for transfers between devices, junction_add(): lax.psum(jnp.dot(onehot.T, end_states, precision=lax.Precision.HIGHEST, p...  326 us
    mul x43, local copies, waits for them, and re-layouts, block_apply(): summed = summed + factor[:, None] * state_in[member][None]  56.6 us
    slice x4, other arithmetic, block_apply(): summed = summed + factor[:, None] * state_in[member][None]  50.6 us
    add x1, other arithmetic, on_device(): result = result + block_apply(right_blocks, downstream, False)  30.5 us
    add x1, other arithmetic, on_device(): result = result + block_apply(right_prev, upstream, True)  30.3 us
  transfers between devices with their start and end apart: 8, of which 2 were waited for; matrix products, arithmetic and copies ran while one was open for 30% of the time, Pallas kernels for 0%

commit v1 on v0

v1 whole, which is shorter than its diff:
```python
import jax
import jax.numpy as jnp
from jax import lax
from jax.experimental import pallas as pl
from jax.experimental.pallas import tpu as pltpu
from jax.sharding import PartitionSpec as P

MESH = pl.DeviceIdType.MESH
HIGH = lax.Precision.HIGHEST
F32 = jnp.float32
X_SIZE, Z_SIZE = 4, 8
COMP, NPAR, COLS, PIPES, CELLS = 4, 2, 64, 8, 256
LANES = 128
Z_STEPS = (4, 3, 5, 2, 6, 1, 7)
PE, PN, DD, CIN, COUT, WT = 0, 8, 16, 32, 48, 64
N_COEF = 68
J_W, J_ONE, J_ID = 24, 28, 29
ROWS = 24


def iota(shape, dim):
    return lax.broadcasted_iota(jnp.int32, shape, dim)


def spread(column):
    return jnp.broadcast_to(column, (PIPES, LANES))


def kernel(
    dir_in, diag_in, left_in, right_in, par_in, wt_in, ids_in, out_ref,
    dirs, diag, left, right, par, wt, ids,
    hess, band, coef, comp, src_s, wl_s, n_send, n_recv, jbuf, mean_s, mean_a,
    in_sem, out_sem, ns_sem, nr_sem, zs_sem, zr_sem, ys_sem, yr_sem,
):
    g = lax.axis_index("region")
    s = lax.axis_index("sub")
    x, z = g // Z_SIZE, lax.rem(g, Z_SIZE)
    is_first, is_last = s == 0, s == 7
    is_end = jnp.logical_or(is_first, is_last)
    pe = s // 7

    z_peers = [(x * Z_SIZE + lax.rem(z + k, Z_SIZE), s) for k in Z_STEPS]
    xr = [lax.rem(x + k, X_SIZE) * Z_SIZE + z for k in range(X_SIZE)]
    y_peers = [(xr[2], 7 - s), (xr[1], 7 - s), (xr[3], 7 - s), (xr[2], s), (xr[1], s), (xr[3], s), (g, 7 - s)]

    def to(peer):
        return dict(device_id={"region": peer[0], "sub": peer[1]}, device_id_type=MESH)

    interior = (s > 0, s < 7)
    beside = ((g, s - 1), (g, s + 1))

    loads = [
        pltpu.make_async_copy(a, b, in_sem.at[i])
        for i, (a, b) in enumerate(
            (
                (dir_in, dirs),
                (diag_in, diag),
                (left_in, left),
                (right_in, right),
                (par_in, par),
                (wt_in, wt),
                (ids_in, ids),
            )
        )
    ]
    for load in loads:
        load.start()
    barrier = pltpu.get_barrier_semaphore()
    for side in (0, 1):

        @pl.when(interior[side])
        def _():
            pl.semaphore_signal(barrier, inc=1, **to(beside[side]))

    @pl.when(is_end)
    def _():
        for peer in z_peers + y_peers:
            pl.semaphore_signal(barrier, inc=1, **to(peer))

    for load in loads:
        load.wait()

    lane = iota((PIPES, LANES), 1)
    even = lax.rem(lane, 2) == 0
    lane2 = iota((PIPES, CELLS), 1)

    ends = jnp.logical_or(
        jnp.logical_and(lane2 == 0, is_first), jnp.logical_and(lane2 == CELLS - 1, is_last)
    )
    for c in range(COMP):
        diag[c, c] = diag[c, c] - jnp.where(ends, 0.5, 0.0)

    def gather_step(j, tiles):
        tiles = list(tiles)
        for u in range(4):
            r = j * 4 + u
            here = lane // 2 == r
            for k in range(NPAR):
                a = dirs[k, r, :, 0:LANES]
                b = dirs[k, r, :, LANES:]
                tiles[k] = jnp.where(here, pltpu.roll(a, 2 * r, 1), tiles[k])
                tiles[2 + k] = jnp.where(here, pltpu.roll(b, lax.rem(2 * r + 2, LANES), 1), tiles[2 + k])
        return tuple(tiles)

    zero = jnp.zeros((PIPES, LANES), F32)
    tiles = lax.fori_loop(0, COLS // 4, gather_step, (zero,) * 4)

    def swap(v):
        return jnp.where(even, pltpu.roll(v, LANES - 1, 1), pltpu.roll(v, 1, 1))

    def nxt(v):
        return pltpu.roll(v, LANES - 1, 1)

    def lane_pack(values):
        tile = jnp.zeros((PIPES, LANES), F32)
        for i, v in enumerate(values):
            tile = jnp.where(lane == i, v, tile)
        return tile

    for side in (0, 1):
        for k in range(NPAR):
            comp[side, k] = swap(tiles[2 + k]) if side else tiles[k]
        e, n = (CELLS - 1, CELLS - 2) if side else (0, 1)
        inner, outer = (left, right) if side else (right, left)
        for t in range(COMP):
            coef[side, WT + t] = spread(wt[t, :, e : e + 1])
            for k in range(NPAR):
                coef[side, PE + NPAR * t + k] = spread(par[t, k, :, e : e + 1])
                coef[side, PN + NPAR * t + k] = spread(par[t, k, :, n : n + 1])
            for q in range(COMP):
                coef[side, DD + COMP * t + q] = spread(diag[t, q, :, e : e + 1])
                coef[side, CIN + COMP * t + q] = spread(inner[t, q, :, e : e + 1])
                coef[side, COUT + COMP * t + q] = spread(outer[t, q, :, e : e + 1])
        source = []
        for t in range(COMP):
            total = zero
            for k in range(NPAR):
                factor = jnp.where(even, coef[side, PE + NPAR * t + k], coef[side, PN + NPAR * t + k])
                total = total + factor * comp[side, k]
            source.append(total)
        after = [nxt(v) for v in source]
        for t in range(COMP):
            total = source[t]
            for q in range(COMP):
                total = total + coef[side, DD + COMP * t + q] * source[q]
                total = total + coef[side, CIN + COMP * t + q] * after[q]
            weighted = coef[side, WT + t] * total
            src_s[side, t] = source[t]
            wl_s[side, t] = weighted
            n_send[side, t] = jnp.where(even, source[t], pltpu.roll(weighted, 1, 1))
        n_send[side, COMP] = lane_pack(
            [coef[side, COUT + i] for i in range(COMP * COMP)] + [coef[side, WT + t] for t in range(COMP)]
        )

    @pl.when(is_end)
    def _():
        row = jnp.where(is_last, ids[1], ids[0])
        row = jnp.where(g >= 16, row[:, LANES:], row[:, :LANES]).astype(F32)
        mine = lane == PIPES * lax.rem(g, 16) + iota((PIPES, LANES), 0)
        own = spread(jnp.sum(jnp.where(mine, row, 0.0), axis=1, keepdims=True))
        pack = [coef[pe, PE + i] for i in range(COMP * NPAR)]
        for near in (True, False):
            for t in range(COMP):
                for k in range(NPAR):
                    total = coef[pe, PE + NPAR * t + k] if near else zero
                    for q in range(COMP):
                        block, cell = (DD, PE) if near else (CIN, PN)
                        total = total + coef[pe, block + COMP * t + q] * coef[pe, cell + NPAR * q + k]
                    pack.append(coef[pe, WT + t] * total)
        pack += [coef[pe, WT + t] for t in range(COMP)] + [zero + 1.0, own]
        for k in range(NPAR):
            jbuf[0, 0, 8 * k : 8 * k + 8] = comp[pe, k]
        jbuf[0, 0, 16:24] = lane_pack(pack)

    expected = jnp.where(is_end, 1 + len(z_peers) + len(y_peers), 2)
    pl.semaphore_wait(barrier, expected)

    def n_copy(side):
        return pltpu.make_async_remote_copy(
            src_ref=n_send.at[side],
            dst_ref=n_recv.at[1 - side],
            send_sem=ns_sem.at[side],
            recv_sem=nr_sem.at[1 - side],
            **to(beside[side]),
        )

    def z_copy(i):
        return pltpu.make_async_remote_copy(
            src_ref=jbuf.at[0, 0], dst_ref=jbuf.at[1 + i, 0], send_sem=zs_sem, recv_sem=zr_sem.at[i], **to(z_peers[i])
        )

    def forward(i):
        for j, peer in enumerate(y_peers):
            pltpu.make_async_remote_copy(
                src_ref=jbuf.at[i, 0], dst_ref=jbuf.at[i, 1 + j], send_sem=ys_sem, recv_sem=yr_sem, **to(peer)
            ).start()

    @pl.when(is_end)
    def _():
        for i in range(len(z_peers)):
            z_copy(i).start()
        forward(0)

    for side in (0, 1):

        @pl.when(interior[side])
        def _():
            n_copy(side).start()

    def up(v):
        return jnp.where(lane2 == CELLS - 1, 0.0, pltpu.roll(v, CELLS - 1, 1))

    def down(v):
        return jnp.where(lane2 == 0, 0.0, pltpu.roll(v, 1, 1))

    p_here = [[par[t, k] for k in range(NPAR)] for t in range(COMP)]
    p_up = [[up(v) for v in vs] for vs in p_here]
    p_down = [[down(v) for v in vs] for vs in p_here]

    def product(blocks, cells, start):
        rows = []
        for t in range(COMP):
            row = []
            for k in range(NPAR):
                total = start[t][k] if start is not None else None
                for q in range(COMP):
                    term = blocks[t, q] * cells[q][k]
                    total = term if total is None else total + term
                row.append(total)
            rows.append(row)
        return rows

    b0 = product(diag, p_here, p_here)
    bm = product(left, p_down, None)
    bp = product(right, p_up, None)
    weight = [wt[t] for t in range(COMP)]
    u0 = [[weight[t] * v for v in b0[t]] for t in range(COMP)]
    um = [[weight[t] * v for v in bm[t]] for t in range(COMP)]
    upl = [[weight[t] * v for v in bp[t]] for t in range(COMP)]

    def inner_sum(a, b, k, q):
        total = a[0][k] * b[0][q]
        for t in range(1, COMP):
            total = total + a[t][k] * b[t][q]
        return total

    for k in range(NPAR):
        for q in range(NPAR):
            i = NPAR * k + q
            if k <= q:
                centre = inner_sum(b0, u0, k, q) + down(inner_sum(bp, upl, k, q)) + up(inner_sum(bm, um, k, q))
                band[8 + i] = centre
                if k != q:
                    band[8 + NPAR * q + k] = centre
            one = inner_sum(b0, upl, k, q) + up(inner_sum(bm, u0, k, q))
            two = up(inner_sum(bm, upl, k, q))
            band[12 + i] = one
            band[16 + i] = two
            band[4 + NPAR * q + k] = down(one)
            band[NPAR * q + k] = down(down(two))

    def wide_step(r, carry):
        shifted = []
        for k in range(NPAR):
            a = dirs[k, r, :, 0:LANES]
            b = dirs[k, r, :, LANES:]
            per_offset = []
            for off in (-2, -1, 0, 1, 2):
                if off == 0:
                    per_offset.append((a, b))
                    continue
                ra = pltpu.roll(a, -off % LANES, 1)
                rb = pltpu.roll(b, -off % LANES, 1)
                if off < 0:
                    per_offset.append((ra, jnp.where(lane < -off, ra, rb)))
                else:
                    per_offset.append((jnp.where(lane >= LANES - off, rb, ra), rb))
            shifted.append(per_offset)
        for half in (0, 1):
            span = slice(half * LANES, half * LANES + LANES)
            for k in range(NPAR):
                total = None
                for o in range(5):
                    for q in range(NPAR):
                        term = band[4 * o + NPAR * k + q, :, span] * shifted[q][o][half]
                        total = term if total is None else total + term
                hess[k, r, :, span] = total
        return carry

    lax.fori_loop(0, COLS, wide_step, 0)

    def finish(side):
        is_right = side == 1
        change = [coef[side, WT + t] * mean_s[side, t] for t in range(COMP)]
        at_end, at_next = [], []
        for q in range(COMP):
            total = change[q] + mean_a[side, q]
            other = zero
            for t in range(COMP):
                total = total + coef[side, DD + COMP * t + q] * change[t]
                other = other + coef[side, CIN + COMP * t + q] * change[t]
            at_end.append(total)
            at_next.append(other)
        corr = []
        for k in range(NPAR):
            c0, c1 = zero, zero
            for t in range(COMP):
                c0 = c0 + coef[side, PE + NPAR * t + k] * at_end[t]
                c1 = c1 + coef[side, PN + NPAR * t + k] * at_next[t]
            straight = jnp.where(even, c0, pltpu.roll(c1, 1, 1))
            corr.append(jnp.where(is_right, swap(straight), straight))
        edge = jnp.where(is_right, LANES - 2, 0)
        here = jnp.logical_and(lane >= edge, lane < edge + 2)
        start = side * LANES
        if not isinstance(side, int):
            start = pl.multiple_of(start, LANES)

        def add_step(j, carry):
            for u in range(4):
                r = j * 4 + u
                for k in range(NPAR):
                    moved = pltpu.roll(corr[k], lax.rem(LANES + edge - 2 * r, LANES), 1)
                    at = (k, r, slice(None), pl.ds(start, LANES))
                    hess[at] = hess[at] + jnp.where(here, moved, 0.0)
            return carry

        lax.fori_loop(0, COLS // 4, add_step, 0)
        half = (slice(None), slice(None), slice(None), pl.ds(start, LANES))
        pltpu.make_async_copy(hess.at[half], out_ref.at[half], out_sem.at[side]).start()

    @pl.when(is_end)
    def _():
        for i in reversed(range(len(z_peers))):
            z_copy(i).wait_recv()
            forward(1 + i)

    for side in (0, 1):

        @pl.when(interior[side])
        def _():
            n_copy(1 - side).wait_recv()
            theirs = n_recv[side, COMP]
            out_block = [spread(theirs[:, i : i + 1]) for i in range(COMP * COMP)]
            out_weight = [spread(theirs[:, COMP * COMP + t : COMP * COMP + t + 1]) for t in range(COMP)]
            pairs = [n_recv[side, t] for t in range(COMP)]
            adjoint = []
            for t in range(COMP):
                total, change = zero, zero
                for q in range(COMP):
                    total = total + out_block[COMP * t + q] * src_s[side, q]
                    change = change + coef[side, COUT + COMP * t + q] * pairs[q]
                adjoint.append(nxt(pairs[t]) + out_weight[t] * total)
                mean_s[side, t] = change
            for q in range(COMP):
                total = zero
                for t in range(COMP):
                    total = total + out_block[COMP * t + q] * adjoint[t]
                mean_a[side, q] = total
            finish(side)

    @pl.when(is_end)
    def _():
        tail = jbuf.at[:, pl.ds(1, 7)]
        arrived = pltpu.make_async_remote_copy(
            src_ref=tail, dst_ref=tail, send_sem=ys_sem, recv_sem=yr_sem, **to(y_peers[0])
        )
        arrived.wait_recv()
        count = 64 * PIPES
        x0 = jbuf[:, :, 0:8].reshape(count, LANES)
        x1 = jbuf[:, :, 8:16].reshape(count, LANES)
        cf = jbuf[:, :, 16:24].reshape(count, LANES)
        replicate = (iota((LANES, 2 * LANES), 0) == iota((LANES, 2 * LANES), 1) // PIPES).astype(F32)
        wide = jnp.dot(cf, replicate, precision=HIGH, preferred_element_type=F32)
        own = cf[0:8, J_ID : J_ID + 1]
        pattern = lax.rem(lane, PIPES) == iota((PIPES, LANES), 0)
        own_lane = jnp.sum(jnp.where(pattern, own, 0.0), axis=0, keepdims=True)
        same = cf[:, J_ID : J_ID + 1] == own_lane
        w0 = jnp.where(same, wide[:, :LANES], 0.0)
        w1 = jnp.where(same, wide[:, LANES:], 0.0)
        w_all = jnp.concatenate([w0, w1], axis=1)
        x_all = jnp.concatenate([x0, x1], axis=1)
        sums = jnp.dot(w_all.T, x_all, precision=HIGH, preferred_element_type=F32)
        totals = jnp.sum(w1, axis=0, keepdims=True)

        def member(i):
            at = lane == PIPES * (i - 16) + iota((PIPES, LANES), 0)
            return spread(jnp.sum(jnp.where(at, totals, 0.0), axis=1, keepdims=True))

        share = 1.0 / member(J_ONE)

        def part(c, k):
            return sums[PIPES * c : PIPES * c + PIPES, LANES * k : LANES * k + LANES]

        for t in range(COMP):
            c = NPAR * t
            mean = share * (part(c, 0) + part(c + 1, 1))
            near = part(8 + c, 0) + part(9 + c, 1)
            far = part(16 + c, 0) + part(17 + c, 1)
            mean_s[pe, t] = 0.5 * mean
            mean_a[pe, t] = 0.5 * share * (near + nxt(far) + 0.5 * member(J_W + t) * mean)
        finish(pe)
        arrived.wait_send()
        pltpu.make_async_remote_copy(
            src_ref=jbuf.at[pl.ds(0, 7), 0],
            dst_ref=jbuf.at[pl.ds(1, 7), 0],
            send_sem=zs_sem,
            recv_sem=yr_sem,
            **to(z_peers[0]),
        ).wait_send()

    for side in (0, 1):

        @pl.when(interior[side])
        def _():
            n_copy(side).wait_send()

    for side in (0, 1):
        span = pl.ds(side * LANES, LANES)
        pltpu.make_async_copy(hess.at[:, :, :, span], out_ref.at[:, :, :, span], out_sem.at[side]).wait()


def on_device(directions, diag_blocks, left_blocks, right_blocks, param_blocks, obs_weight, end_junction):
    args = (directions, diag_blocks, left_blocks, right_blocks, param_blocks, obs_weight, jnp.swapaxes(end_junction, 1, 2))
    dma = pltpu.SemaphoreType.DMA
    return pl.pallas_call(
        kernel,
        out_shape=jax.ShapeDtypeStruct(directions.shape, F32),
        in_specs=[pl.BlockSpec(memory_space=pl.ANY)] * len(args),
        out_specs=pl.BlockSpec(memory_space=pl.ANY),
        scratch_shapes=[pltpu.VMEM(a.shape, a.dtype) for a in args]
        + [
            pltpu.VMEM(directions.shape, F32),
            pltpu.VMEM((5 * NPAR * NPAR, PIPES, CELLS), F32),
            pltpu.VMEM((2, N_COEF, PIPES, LANES), F32),
            pltpu.VMEM((2, NPAR, PIPES, LANES), F32),
            pltpu.VMEM((2, COMP, PIPES, LANES), F32),
            pltpu.VMEM((2, COMP, PIPES, LANES), F32),
            pltpu.VMEM((2, COMP + 1, PIPES, LANES), F32),
            pltpu.VMEM((2, COMP + 1, PIPES, LANES), F32),
            pltpu.VMEM((8, 8, ROWS, LANES), F32),
            pltpu.VMEM((2, COMP, PIPES, LANES), F32),
            pltpu.VMEM((2, COMP, PIPES, LANES), F32),
            dma((7,)),
            dma((2,)),
            dma((2,)),
            dma((2,)),
            dma,
            dma((7,)),
            dma,
            dma,
        ],
        compiler_params=pltpu.CompilerParams(
            collective_id=3, has_side_effects=True, vmem_limit_bytes=40 * 1024 * 1024
        ),
    )(*args)


def solution(mesh):
    return jax.shard_map(
        on_device,
        mesh=mesh,
        in_specs=(
            P(None, None, "region", "sub"),
            P(None, None, "region", "sub"),
            P(None, None, "region", "sub"),
            P(None, None, "region", "sub"),
            P(None, None, "region", "sub"),
            P(None, "region", "sub"),
            P(),
        ),
        out_specs=P(None, None, "region", "sub"),
        check_vma=False,
    )
```

time: 580 us -> 33.1 us (0.06)
  waiting for transfers between devices: 326 us -> 0 us
  other arithmetic: 139 us -> 0 us
  local copies, waits for them, and re-layouts: 77.9 us -> 7.19 us
  Pallas kernels: 0 us -> 25.6 us
  starting transfers between devices: 14.7 us -> 0 us
  between operations: 13.7 us -> 0.02 us
    psum x2 -> x0, waiting for transfers between devices: 326 us -> none  [junction_add(): lax.psum(jnp.dot(onehot.T, end_states, precision=lax.Precision.HIGHEST, p...]
    add x4 -> x0, other arithmetic: 70.1 us -> none  [the longest x1 30.5 us: on_device(): result = result + block_apply(right_blocks, downstream, False)]
    mul x43 -> x0, local copies, waits for them, and re-layouts: 56.6 us -> none  [block_apply(): summed = summed + factor[:, None] * state_in[member][None]]
    slice x4 -> x0, other arithmetic: 50.6 us -> none  [block_apply(): summed = summed + factor[:, None] * state_in[member][None]]
    pallas_call x0 -> x1, Pallas kernels: none -> 25.6 us  [on_device(): pl.pallas_call(kernel, out_shape=jax.ShapeDtypeStruct(directions.shape, F...]
    ppermute x6 -> x0, starting transfers between devices: 14.6 us -> none  [the longest x2 7 us: padded_2(): lax.ppermute(tail, axis, [(i, (i + 1) % count) for i in range(ends)])]
    slice x5 -> x0, local copies, waits for them, and re-layouts: 13.9 us -> none  [the longest x1 11.3 us: block_apply(): summed = summed + factor[:, None] * state_in[member][None]]
    mul x3 -> x0, other arithmetic: 10.9 us -> none  [the longest x1 9.22 us: on_device(): adjoint = obs_weight[:, None] * state]
  transfers between devices with their start and end apart: 8 -> 0, of which waited for: 2 -> 0; matrix products, arithmetic and copies ran while one was open for 30% -> 0% of each run, Pallas kernels for 0% -> 0%
where the time goes in v1:
time: 33.1 us; the launch traced here: 32.8 us
  Pallas kernels  25.6 us (77%)
  local copies, waits for them, and re-layouts  7.19 us (22%)
    pallas_call x1, Pallas kernels, on_device(): pl.pallas_call(kernel, out_shape=jax.ShapeDtypeStruct(directions.shape, F...  25.6 us
    unnamed x15, local copies, waits for them, and re-layouts  7.19 us

profile of v1, /device:TPU:32, one launch (start us, length us, event | category | flops | bytes accessed | tf_op | source)
XLA Modules:
  0.0 32.8 jit_solution(2241000787490829130)
XLA Ops:
  0.0 0.0 copy-start
  0.0 1.2 %copy-done = f32[2,64,8,256]{3,2,1,0:T(8,128)S(1)} copy-done((f32[2,64,8,256]{3,2,1,0:T(8,128)S(1)}, f32[2,64,8,256]{3,2,1,0:T(8,128)}, u32[]{:S(2)}) %copy-start) | copy-done | bytes 1048600
  1.2 0.0 copy-start.1
  1.2 0.9 %copy-done.1 = f32[4,4,8,256]{3,2,1,0:T(8,128)S(1)} copy-done((f32[4,4,8,256]{3,2,1,0:T(8,128)S(1)}, f32[4,4,8,256]{3,2,1,0:T(8,128)}, u32[]{:S(2)}) %copy-start.1) | copy-done | bytes 131096
  2.1 0.0 copy-start.2
  2.1 0.9 %copy-done.2 = f32[4,4,8,256]{3,2,1,0:T(8,128)S(1)} copy-done((f32[4,4,8,256]{3,2,1,0:T(8,128)S(1)}, f32[4,4,8,256]{3,2,1,0:T(8,128)}, u32[]{:S(2)}) %copy-start.2) | copy-done | bytes 131096
  3.0 0.0 copy-start.3
  3.0 0.9 %copy-done.3 = f32[4,4,8,256]{3,2,1,0:T(8,128)S(1)} copy-done((f32[4,4,8,256]{3,2,1,0:T(8,128)S(1)}, f32[4,4,8,256]{3,2,1,0:T(8,128)}, u32[]{:S(2)}) %copy-start.3) | copy-done | bytes 131096
  3.9 0.0 copy-start.4
  3.9 0.8 %copy-done.4 = f32[4,2,8,256]{3,2,1,0:T(8,128)S(1)} copy-done((f32[4,2,8,256]{3,2,1,0:T(8,128)S(1)}, f32[4,2,8,256]{3,2,1,0:T(8,128)}, u32[]{:S(2)}) %copy-start.4) | copy-done | bytes 65560
  4.8 0.0 copy-start.5
  4.8 0.8 %copy-done.5 = f32[4,8,256]{2,1,0:T(8,128)S(1)} copy-done((f32[4,8,256]{2,1,0:T(8,128)S(1)}, f32[4,8,256]{2,1,0:T(8,128)}, u32[]{:S(2)}) %copy-start.5) | copy-done | bytes 32792
  5.5 0.0 copy-start.6
  5.5 0.7 %copy-done.6 = s32[2,256,1]{1,2,0:T(1,128)S(1)} copy-done((s32[2,256,1]{1,2,0:T(1,128)S(1)}, s32[2,256,1]{1,2,0:T(1,128)}, u32[]{:S(2)}) %copy-start.6) | copy-done | bytes 2072
  6.2 25.6 %shard_map.73 = f32[2,64,8,256]{3,2,1,0:T(8,128)S(1)} custom-call(f32[2,64,8,256]{3,2,1,0:T(8,128)S(1)} %copy-done, f32[4,4,8,256]{3,2,1,0:T(8,128)S(1)} %copy-done.1, f32[4,4,8,256]{3,2,1,0:T(8,128)S(1)} %copy-done.2, f32[4,4,8,256]{3,2,1,0:T(8,128)S(1)} %copy-done.3, f32[4,2,8,256]{3,2,1,0:T(8,128)S(1)} %copy-done.4, f32[4,8,256]{2,1,0:T(8,128)S(1)} %copy-done.5, ...), custom_call_target="tpu_custom_call" | custom-call | tf_op jit(solution)/shard_map/pallas_call | solution.py:425
  31.8 1.0 %copy.9 = f32[2,64,8,256]{3,2,1,0:T(8,128)} copy(f32[2,64,8,256]{3,2,1,0:T(8,128)S(1)} %shard_map.73) | data formatting | bytes 2097152
Async XLA Ops:
  0.0 1.2 %copy-start = (f32[2,64,8,256]{3,2,1,0:T(8,128)S(1)}, f32[2,64,8,256]{3,2,1,0:T(8,128)}, u32[]{:S(2)}) copy-start(f32[2,64,8,256]{3,2,1,0:T(8,128)} %dir_in.1) | copy-start | bytes 3145732
  1.2 0.9 %copy-start.1 = (f32[4,4,8,256]{3,2,1,0:T(8,128)S(1)}, f32[4,4,8,256]{3,2,1,0:T(8,128)}, u32[]{:S(2)}) copy-start(f32[4,4,8,256]{3,2,1,0:T(8,128)} %diag_in.1) | copy-start | bytes 393220
  2.1 0.9 %copy-start.2 = (f32[4,4,8,256]{3,2,1,0:T(8,128)S(1)}, f32[4,4,8,256]{3,2,1,0:T(8,128)}, u32[]{:S(2)}) copy-start(f32[4,4,8,256]{3,2,1,0:T(8,128)} %left_in.1) | copy-start | bytes 393220
  3.0 0.9 %copy-start.3 = (f32[4,4,8,256]{3,2,1,0:T(8,128)S(1)}, f32[4,4,8,256]{3,2,1,0:T(8,128)}, u32[]{:S(2)}) copy-start(f32[4,4,8,256]{3,2,1,0:T(8,128)} %right_in.1) | copy-start | bytes 393220
  3.9 0.8 %copy-start.4 = (f32[4,2,8,256]{3,2,1,0:T(8,128)S(1)}, f32[4,2,8,256]{3,2,1,0:T(8,128)}, u32[]{:S(2)}) copy-start(f32[4,2,8,256]{3,2,1,0:T(8,128)} %par_in.1) | copy-start | bytes 196612
  4.8 0.8 %copy-start.5 = (f32[4,8,256]{2,1,0:T(8,128)S(1)}, f32[4,8,256]{2,1,0:T(8,128)}, u32[]{:S(2)}) copy-start(f32[4,8,256]{2,1,0:T(8,128)} %wt_in.1) | copy-start | bytes 98308
  5.5 0.7 %copy-start.6 = (s32[2,256,1]{1,2,0:T(1,128)S(1)}, s32[2,256,1]{1,2,0:T(1,128)}, u32[]{:S(2)}) copy-start(s32[2,256,1]{1,2,0:T(1,128)} %param.13) | copy-start | bytes 6148

commit v2 on v1

--- a/solution.py
+++ b/solution.py
@@ -27,10 +27,10 @@
 
 
 def kernel(
-    dir_in, diag_in, left_in, right_in, par_in, wt_in, ids_in, out_ref,
+    dir_in, diag_in, left_in, right_in, par_in, wt_in, ids_in, hess,
     dirs, diag, left, right, par, wt, ids,
-    hess, band, coef, comp, src_s, wl_s, n_send, n_recv, jbuf, mean_s, mean_a,
-    in_sem, out_sem, ns_sem, nr_sem, zs_sem, zr_sem, ys_sem, yr_sem,
+    band, coef, comp, src_s, n_send, n_recv, jbuf, mean_s, mean_a,
+    dir_sem, in_sem, ns_sem, nr_sem, zs_sem, zr_sem, ys_sem, yr_sem,
 ):
     g = lax.axis_index("region")
     s = lax.axis_index("sub")
@@ -49,40 +49,40 @@
     interior = (s > 0, s < 7)
     beside = ((g, s - 1), (g, s + 1))
 
+    def half_load(half):
+        start = pl.multiple_of(half * LANES, LANES)
+        return pltpu.make_async_copy(dir_in.at[:, :, :, pl.ds(start, LANES)], dirs.at[half], dir_sem.at[half])
+
     loads = [
         pltpu.make_async_copy(a, b, in_sem.at[i])
         for i, (a, b) in enumerate(
-            (
-                (dir_in, dirs),
-                (diag_in, diag),
-                (left_in, left),
-                (right_in, right),
-                (par_in, par),
-                (wt_in, wt),
-                (ids_in, ids),
-            )
+            ((par_in, par), (diag_in, diag), (wt_in, wt), (left_in, left), (right_in, right), (ids_in, ids))
         )
     ]
+    half_load(pe).start()
     for load in loads:
         load.start()
     barrier = pltpu.get_barrier_semaphore()
+
+    @pl.when(is_end)
+    def _():
+        for peer in z_peers + y_peers:
+            pl.semaphore_signal(barrier, inc=1, **to(peer))
+
     for side in (0, 1):
 
         @pl.when(interior[side])
         def _():
             pl.semaphore_signal(barrier, inc=1, **to(beside[side]))
 
-    @pl.when(is_end)
-    def _():
-        for peer in z_peers + y_peers:
-            pl.semaphore_signal(barrier, inc=1, **to(peer))
-
+    half_load(1 - pe).start()
     for load in loads:
         load.wait()
 
     lane = iota((PIPES, LANES), 1)
     even = lax.rem(lane, 2) == 0
     lane2 = iota((PIPES, CELLS), 1)
+    zero = jnp.zeros((PIPES, LANES), F32)
 
     ends = jnp.logical_or(
         jnp.logical_and(lane2 == 0, is_first), jnp.logical_and(lane2 == CELLS - 1, is_last)
@@ -90,21 +90,6 @@
     for c in range(COMP):
         diag[c, c] = diag[c, c] - jnp.where(ends, 0.5, 0.0)
 
-    def gather_step(j, tiles):
-        tiles = list(tiles)
-        for u in range(4):
-            r = j * 4 + u
-            here = lane // 2 == r
-            for k in range(NPAR):
-                a = dirs[k, r, :, 0:LANES]
-                b = dirs[k, r, :, LANES:]
-                tiles[k] = jnp.where(here, pltpu.roll(a, 2 * r, 1), tiles[k])
-                tiles[2 + k] = jnp.where(here, pltpu.roll(b, lax.rem(2 * r + 2, LANES), 1), tiles[2 + k])
-        return tuple(tiles)
-
-    zero = jnp.zeros((PIPES, LANES), F32)
-    tiles = lax.fori_loop(0, COLS // 4, gather_step, (zero,) * 4)
-
     def swap(v):
         return jnp.where(even, pltpu.roll(v, LANES - 1, 1), pltpu.roll(v, 1, 1))
 
@@ -112,14 +97,24 @@
         return pltpu.roll(v, LANES - 1, 1)
 
     def lane_pack(values):
-        tile = jnp.zeros((PIPES, LANES), F32)
+        tile = zero
         for i, v in enumerate(values):
             tile = jnp.where(lane == i, v, tile)
         return tile
 
-    for side in (0, 1):
+    def end_cells(side):
+        def step(j, tiles):
+            tiles = list(tiles)
+            for u in range(4):
+                r = j * 4 + u
+                shift = lax.rem(2 * r + 2 * side, LANES)
+                for k in range(NPAR):
+                    tiles[k] = jnp.where(lane // 2 == r, pltpu.roll(dirs[side, k, r], shift, 1), tiles[k])
+            return tuple(tiles)
+
+        tiles = lax.fori_loop(0, COLS // 4, step, (zero,) * NPAR, unroll=4)
         for k in range(NPAR):
-            comp[side, k] = swap(tiles[2 + k]) if side else tiles[k]
+            comp[side, k] = swap(tiles[k]) if side else tiles[k]
         e, n = (CELLS - 1, CELLS - 2) if side else (0, 1)
         inner, outer = (left, right) if side else (right, left)
         for t in range(COMP):
@@ -131,46 +126,32 @@
                 coef[side, DD + COMP * t + q] = spread(diag[t, q, :, e : e + 1])
                 coef[side, CIN + COMP * t + q] = spread(inner[t, q, :, e : e + 1])
                 coef[side, COUT + COMP * t + q] = spread(outer[t, q, :, e : e + 1])
-        source = []
-        for t in range(COMP):
-            total = zero
+
+    @pl.when(is_end)
+    def _():
+        half_load(pe).wait()
+
+    for side, chosen in ((0, is_first), (1, is_last)):
+
+        @pl.when(chosen)
+        def _():
+            end_cells(side)
+            row = jnp.where(g >= 16, ids[side, :, LANES:], ids[side, :, :LANES]).astype(F32)
+            mine = lane == PIPES * lax.rem(g, 16) + iota((PIPES, LANES), 0)
+            own = spread(jnp.sum(jnp.where(mine, row, 0.0), axis=1, keepdims=True))
+            pack = [coef[side, PE + i] for i in range(COMP * NPAR)]
+            for near in (True, False):
+                for t in range(COMP):
+                    for k in range(NPAR):
+                        total = coef[side, PE + NPAR * t + k] if near else zero
+                        for q in range(COMP):
+                            block, cell = (DD, PE) if near else (CIN, PN)
+                            total = total + coef[side, block + COMP * t + q] * coef[side, cell + NPAR * q + k]
+                        pack.append(coef[side, WT + t] * total)
+            pack += [coef[side, WT + t] for t in range(COMP)] + [zero + 1.0, own]
             for k in range(NPAR):
-                factor = jnp.where(even, coef[side, PE + NPAR * t + k], coef[side, PN + NPAR * t + k])
-                total = total + factor * comp[side, k]
-            source.append(total)
-        after = [nxt(v) for v in source]
-        for t in range(COMP):
-            total = source[t]
-            for q in range(COMP):
-                total = total + coef[side, DD + COMP * t + q] * source[q]
-                total = total + coef[side, CIN + COMP * t + q] * after[q]
-            weighted = coef[side, WT + t] * total
-            src_s[side, t] = source[t]
-            wl_s[side, t] = weighted
-            n_send[side, t] = jnp.where(even, source[t], pltpu.roll(weighted, 1, 1))
-        n_send[side, COMP] = lane_pack(
-            [coef[side, COUT + i] for i in range(COMP * COMP)] + [coef[side, WT + t] for t in range(COMP)]
-        )
-
-    @pl.when(is_end)
-    def _():
-        row = jnp.where(is_last, ids[1], ids[0])
-        row = jnp.where(g >= 16, row[:, LANES:], row[:, :LANES]).astype(F32)
-        mine = lane == PIPES * lax.rem(g, 16) + iota((PIPES, LANES), 0)
-        own = spread(jnp.sum(jnp.where(mine, row, 0.0), axis=1, keepdims=True))
-        pack = [coef[pe, PE + i] for i in range(COMP * NPAR)]
-        for near in (True, False):
-            for t in range(COMP):
-                for k in range(NPAR):
-                    total = coef[pe, PE + NPAR * t + k] if near else zero
-                    for q in range(COMP):
-                        block, cell = (DD, PE) if near else (CIN, PN)
-                        total = total + coef[pe, block + COMP * t + q] * coef[pe, cell + NPAR * q + k]
-                    pack.append(coef[pe, WT + t] * total)
-        pack += [coef[pe, WT + t] for t in range(COMP)] + [zero + 1.0, own]
-        for k in range(NPAR):
-            jbuf[0, 0, 8 * k : 8 * k + 8] = comp[pe, k]
-        jbuf[0, 0, 16:24] = lane_pack(pack)
+                jbuf[0, 0, 8 * k : 8 * k + 8] = comp[side, k]
+            jbuf[0, 0, 16:24] = lane_pack(pack)
 
     expected = jnp.where(is_end, 1 + len(z_peers) + len(y_peers), 2)
     pl.semaphore_wait(barrier, expected)
@@ -201,10 +182,35 @@
             z_copy(i).start()
         forward(0)
 
+    half_load(1 - pe).wait()
+
+    @pl.when(jnp.logical_not(is_end))
+    def _():
+        half_load(pe).wait()
+
     for side in (0, 1):
 
         @pl.when(interior[side])
         def _():
+            end_cells(side)
+            source = []
+            for t in range(COMP):
+                total = zero
+                for k in range(NPAR):
+                    factor = jnp.where(even, coef[side, PE + NPAR * t + k], coef[side, PN + NPAR * t + k])
+                    total = total + factor * comp[side, k]
+                source.append(total)
+            after = [nxt(v) for v in source]
+            for t in range(COMP):
+                total = source[t]
+                for q in range(COMP):
+                    total = total + coef[side, DD + COMP * t + q] * source[q]
+                    total = total + coef[side, CIN + COMP * t + q] * after[q]
+                src_s[side, t] = source[t]
+                n_send[side, t] = jnp.where(even, source[t], pltpu.roll(coef[side, WT + t] * total, 1, 1))
+            n_send[side, COMP] = lane_pack(
+                [coef[side, COUT + i] for i in range(COMP * COMP)] + [coef[side, WT + t] for t in range(COMP)]
+            )
             n_copy(side).start()
 
     def up(v):
@@ -262,8 +268,8 @@
     def wide_step(r, carry):
         shifted = []
         for k in range(NPAR):
-            a = dirs[k, r, :, 0:LANES]
-            b = dirs[k, r, :, LANES:]
+            a = dirs[0, k, r]
+            b = dirs[1, k, r]
             per_offset = []
             for off in (-2, -1, 0, 1, 2):
                 if off == 0:
@@ -287,7 +293,7 @@
                 hess[k, r, :, span] = total
         return carry
 
-    lax.fori_loop(0, COLS, wide_step, 0)
+    lax.fori_loop(0, COLS, wide_step, 0, unroll=4)
 
     def finish(side):
         is_right = side == 1
@@ -324,9 +330,7 @@
                     hess[at] = hess[at] + jnp.where(here, moved, 0.0)
             return carry
 
-        lax.fori_loop(0, COLS // 4, add_step, 0)
-        half = (slice(None), slice(None), slice(None), pl.ds(start, LANES))
-        pltpu.make_async_copy(hess.at[half], out_ref.at[half], out_sem.at[side]).start()
+        lax.fori_loop(0, COLS // 4, add_step, 0, unroll=4)
 
     @pl.when(is_end)
     def _():
@@ -366,25 +370,15 @@
         )
         arrived.wait_recv()
         count = 64 * PIPES
-        x0 = jbuf[:, :, 0:8].reshape(count, LANES)
-        x1 = jbuf[:, :, 8:16].reshape(count, LANES)
-        cf = jbuf[:, :, 16:24].reshape(count, LANES)
-        replicate = (iota((LANES, 2 * LANES), 0) == iota((LANES, 2 * LANES), 1) // PIPES).astype(F32)
-        wide = jnp.dot(cf, replicate, precision=HIGH, preferred_element_type=F32)
-        own = cf[0:8, J_ID : J_ID + 1]
-        pattern = lax.rem(lane, PIPES) == iota((PIPES, LANES), 0)
-        own_lane = jnp.sum(jnp.where(pattern, own, 0.0), axis=0, keepdims=True)
-        same = cf[:, J_ID : J_ID + 1] == own_lane
-        w0 = jnp.where(same, wide[:, :LANES], 0.0)
-        w1 = jnp.where(same, wide[:, LANES:], 0.0)
-        w_all = jnp.concatenate([w0, w1], axis=1)
-        x_all = jnp.concatenate([x0, x1], axis=1)
-        sums = jnp.dot(w_all.T, x_all, precision=HIGH, preferred_element_type=F32)
-        totals = jnp.sum(w1, axis=0, keepdims=True)
+        x_all = jnp.concatenate([jbuf[:, :, 0:8].reshape(count, LANES), jbuf[:, :, 8:16].reshape(count, LANES)], axis=1)
+        coefs = jbuf[:, :, 16:24].reshape(count, LANES).T
+        own = spread(jbuf[0, 0, 16:24, J_ID : J_ID + 1])[:, 0:1]
+        same = coefs[J_ID : J_ID + 1] == own
+        rows = [jnp.where(same, coefs[i : i + 1], 0.0) for i in range(J_ONE + 1)]
+        sums = jnp.dot(jnp.concatenate(rows[:J_W]), x_all, precision=HIGH, preferred_element_type=F32)
 
         def member(i):
-            at = lane == PIPES * (i - 16) + iota((PIPES, LANES), 0)
-            return spread(jnp.sum(jnp.where(at, totals, 0.0), axis=1, keepdims=True))
+            return spread(jnp.sum(rows[i], axis=1, keepdims=True))
 
         share = 1.0 / member(J_ONE)
 
@@ -414,34 +408,34 @@
         def _():
             n_copy(side).wait_send()
 
-    for side in (0, 1):
-        span = pl.ds(side * LANES, LANES)
-        pltpu.make_async_copy(hess.at[:, :, :, span], out_ref.at[:, :, :, span], out_sem.at[side]).wait()
-
 
 def on_device(directions, diag_blocks, left_blocks, right_blocks, param_blocks, obs_weight, end_junction):
     args = (directions, diag_blocks, left_blocks, right_blocks, param_blocks, obs_weight, jnp.swapaxes(end_junction, 1, 2))
+    args = tuple(pltpu.with_memory_space_constraint(a, pltpu.HBM) for a in args)
     dma = pltpu.SemaphoreType.DMA
+
+    def tiles(*counts):
+        return pltpu.VMEM(counts + (PIPES, LANES), F32)
+
     return pl.pallas_call(
         kernel,
-        out_shape=jax.ShapeDtypeStruct(directions.shape, F32),
+        out_shape=pltpu.VMEM(directions.shape, F32),
         in_specs=[pl.BlockSpec(memory_space=pl.ANY)] * len(args),
-        out_specs=pl.BlockSpec(memory_space=pl.ANY),
-        scratch_shapes=[pltpu.VMEM(a.shape, a.dtype) for a in args]
+        out_specs=pl.BlockSpec(memory_space=pltpu.VMEM),
+        scratch_shapes=[tiles(2, NPAR, COLS)]
+        + [pltpu.VMEM(a.shape, a.dtype) for a in args[1:]]
         + [
-            pltpu.VMEM(directions.shape, F32),
             pltpu.VMEM((5 * NPAR * NPAR, PIPES, CELLS), F32),
-            pltpu.VMEM((2, N_COEF, PIPES, LANES), F32),
-            pltpu.VMEM((2, NPAR, PIPES, LANES), F32),
-            pltpu.VMEM((2, COMP, PIPES, LANES), F32),
-            pltpu.VMEM((2, COMP, PIPES, LANES), F32),
-            pltpu.VMEM((2, COMP + 1, PIPES, LANES), F32),
-            pltpu.VMEM((2, COMP + 1, PIPES, LANES), F32),
+            tiles(2, N_COEF),
+            tiles(2, NPAR),
+            tiles(2, COMP),
+            tiles(2, COMP + 1),
+            tiles(2, COMP + 1),
             pltpu.VMEM((8, 8, ROWS, LANES), F32),
-            pltpu.VMEM((2, COMP, PIPES, LANES), F32),
-            pltpu.VMEM((2, COMP, PIPES, LANES), F32),
-            dma((7,)),
+            tiles(2, COMP),
+            tiles(2, COMP),
             dma((2,)),
+            dma((6,)),
             dma((2,)),
             dma((2,)),
             dma,
@@ -450,7 +444,7 @@
             dma,
         ],
         compiler_params=pltpu.CompilerParams(
-            collective_id=3, has_side_effects=True, vmem_limit_bytes=40 * 1024 * 1024
+            collective_id=3, has_side_effects=True, vmem_limit_bytes=56 * 1024 * 1024
         ),
     )(*args)
 

time: 33.1 us -> 21.1 us (0.64)
  local copies, waits for them, and re-layouts: 7.19 us -> 0.97 us
  Pallas kernels: 25.6 us -> 20 us
    unnamed x15 -> x1, local copies, waits for them, and re-layouts: 7.19 us -> 0.97 us
    pallas_call x1, Pallas kernels: 25.6 us -> 20 us  [on_device(): pl.pallas_call(kernel, out_shape=pltpu.VMEM(directions.shape, F32), in_sp...]
where the time goes in v2:
time: 21.1 us; the launch traced here: 21 us
  Pallas kernels  20 us (95%)
  local copies, waits for them, and re-layouts  0.97 us (5%)
    pallas_call x1, Pallas kernels, on_device(): pl.pallas_call(kernel, out_shape=pltpu.VMEM(directions.shape, F32), in_sp...  20 us
    unnamed x1, local copies, waits for them, and re-layouts  0.97 us

profile of v2, /device:TPU:32, one launch (start us, length us, event | category | flops | bytes accessed | tf_op | source)
XLA Modules:
  0.0 21.0 jit_solution(9165954641064453036)
XLA Ops:
  0.0 20.0 %shard_map.73 = f32[2,64,8,256]{3,2,1,0:T(8,128)S(1)} custom-call(f32[2,64,8,256]{3,2,1,0:T(8,128)} %dir_in.1, f32[4,4,8,256]{3,2,1,0:T(8,128)} %diag_in.1, f32[4,4,8,256]{3,2,1,0:T(8,128)} %left_in.1, f32[4,4,8,256]{3,2,1,0:T(8,128)} %right_in.1, f32[4,2,8,256]{3,2,1,0:T(8,128)} %par_in.1, f32[4,8,256]{2,1,0:T(8,128)} %wt_in.1, s32[2,1,256]{2,1,0:T(1,128)} %bitcast.1), custom_call_target="tpu_custom_call" | custom-call | tf_op jit(solution)/shard_map/pallas_call | solution.py:420
  20.0 1.0 %copy.9 = f32[2,64,8,256]{3,2,1,0:T(8,128)} copy(f32[2,64,8,256]{3,2,1,0:T(8,128)S(1)} %shard_map.73) | data formatting | bytes 2097152

commit v3 on v2

v3 whole, which is shorter than its diff:
```python
import jax
import jax.numpy as jnp
from jax import lax
from jax.experimental import pallas as pl
from jax.experimental.pallas import tpu as pltpu
from jax.sharding import PartitionSpec as P

MESH = pl.DeviceIdType.MESH
F32 = jnp.float32
BF16 = jnp.bfloat16
X_SIZE, Z_SIZE = 4, 8
COMP, NPAR, COLS, PIPES, CELLS = 4, 2, 64, 8, 256
LANES = 128
Z_STEPS = (4, 3, 5, 2, 6, 1, 7)
PE, PN, DD, CIN, COUT, WT = 0, 8, 16, 32, 48, 64
N_COEF = 68
J_W, J_ID, J_SPAN = 24, 28, 32
ROWS = 18


def iota(shape, dim):
    return lax.broadcasted_iota(jnp.int32, shape, dim)


def split(v, kind=BF16):
    parts = []
    for _ in range(3):
        part = v.astype(BF16)
        v = v - part.astype(F32)
        parts.append(part.astype(kind))
    return parts


def spread(column):
    return jnp.broadcast_to(column, (PIPES, LANES))


def kernel(
    dir_in, diag_in, left_in, right_in, par_in, wt_in, ids_in, hess,
    dirs, diag, left, right, par, wt, ids,
    band, coef, comp, src_s, n_send, n_recv, jbuf, j_sum, j_weight, j_own, mean_s, mean_a,
    dir_sem, in_sem, ns_sem, nr_sem, zs_sem, zr_sem, ys_sem, yr_sem,
):
    g = lax.axis_index("region")
    s = lax.axis_index("sub")
    x, z = g // Z_SIZE, lax.rem(g, Z_SIZE)
    me = 2 * x + s // 7
    is_first, is_last = s == 0, s == 7
    is_end = jnp.logical_or(is_first, is_last)
    early = jnp.logical_and(is_end, z < Z_SIZE // 2)
    pe = s // 7

    z_peers = [(x * Z_SIZE + lax.rem(z + k, Z_SIZE), s) for k in Z_STEPS]
    xr = [lax.rem(x + k, X_SIZE) * Z_SIZE + z for k in range(X_SIZE)]
    y_peers = [(xr[2], 7 - s), (xr[1], 7 - s), (xr[3], 7 - s), (xr[2], s), (xr[1], s), (xr[3], s), (g, 7 - s)]

    def to(peer):
        return dict(device_id={"region": peer[0], "sub": peer[1]}, device_id_type=MESH)

    interior = (s > 0, s < 7)
    beside = ((g, s - 1), (g, s + 1))

    def half_load(half):
        start = pl.multiple_of(half * LANES, LANES)
        return pltpu.make_async_copy(dir_in.at[:, :, :, pl.ds(start, LANES)], dirs.at[half], dir_sem.at[half])

    loads = [
        pltpu.make_async_copy(a, b, in_sem.at[i])
        for i, (a, b) in enumerate(
            ((par_in, par), (diag_in, diag), (wt_in, wt), (left_in, left), (right_in, right), (ids_in, ids))
        )
    ]
    barrier = pltpu.get_barrier_semaphore()

    @pl.when(is_end)
    def _():
        for peer in z_peers + y_peers:
            pl.semaphore_signal(barrier, inc=1, **to(peer))

    for side in (0, 1):

        @pl.when(interior[side])
        def _():
            pl.semaphore_signal(barrier, inc=1, **to(beside[side]))

    half_load(pe).start()
    for load in loads:
        load.start()
    half_load(1 - pe).start()
    for load in loads:
        load.wait()

    lane = iota((PIPES, LANES), 1)
    even = lax.rem(lane, 2) == 0
    lane2 = iota((PIPES, CELLS), 1)
    quarter = lax.rem(iota((PIPES, LANES), 0), 4)
    zero = jnp.zeros((PIPES, LANES), F32)

    ends = jnp.logical_or(
        jnp.logical_and(lane2 == 0, is_first), jnp.logical_and(lane2 == CELLS - 1, is_last)
    )
    for c in range(COMP):
        diag[c, c] = diag[c, c] - jnp.where(ends, 0.5, 0.0)

    def swap(v):
        return jnp.where(even, pltpu.roll(v, LANES - 1, 1), pltpu.roll(v, 1, 1))

    def nxt(v):
        return pltpu.roll(v, LANES - 1, 1)

    def lane_pack(values):
        tile = zero
        for i, v in enumerate(values):
            tile = jnp.where(lane == i, v, tile)
        return tile

    def end_cells(side):
        def step(j, tiles):
            tiles = list(tiles)
            for u in range(4):
                r = j * 4 + u
                shift = lax.rem(2 * r + 2 * side, LANES)
                for k in range(NPAR):
                    tiles[k] = jnp.where(lane // 2 == r, pltpu.roll(dirs[side, k, r], shift, 1), tiles[k])
            return tuple(tiles)

        tiles = lax.fori_loop(0, COLS // 4, step, (zero,) * NPAR, unroll=4)
        for k in range(NPAR):
            comp[side, k] = swap(tiles[k]) if side else tiles[k]
        e, n = (CELLS - 1, CELLS - 2) if side else (0, 1)
        inner, outer = (left, right) if side else (right, left)
        for t in range(COMP):
            coef[side, WT + t] = spread(wt[t, :, e : e + 1])
            for k in range(NPAR):
                coef[side, PE + NPAR * t + k] = spread(par[t, k, :, e : e + 1])
                coef[side, PN + NPAR * t + k] = spread(par[t, k, :, n : n + 1])
            for q in range(COMP):
                coef[side, DD + COMP * t + q] = spread(diag[t, q, :, e : e + 1])
                coef[side, CIN + COMP * t + q] = spread(inner[t, q, :, e : e + 1])
                coef[side, COUT + COMP * t + q] = spread(outer[t, q, :, e : e + 1])

    @pl.when(is_end)
    def _():
        half_load(pe).wait()

    for side, chosen in ((0, is_first), (1, is_last)):

        @pl.when(chosen)
        def _():
            end_cells(side)
            row = jnp.where(g >= 16, ids[side, :, LANES:], ids[side, :, :LANES]).astype(F32)
            mine = lane == PIPES * lax.rem(g, 16) + iota((PIPES, LANES), 0)
            own = spread(jnp.sum(jnp.where(mine, row, 0.0), axis=1, keepdims=True))
            pack = [coef[side, PE + i] for i in range(COMP * NPAR)]
            for near in (True, False):
                for t in range(COMP):
                    for k in range(NPAR):
                        total = coef[side, PE + NPAR * t + k] if near else zero
                        for q in range(COMP):
                            block, cell = (DD, PE) if near else (CIN, PN)
                            total = total + coef[side, block + COMP * t + q] * coef[side, cell + NPAR * q + k]
                        pack.append(coef[side, WT + t] * total)
            pack += [coef[side, WT + t] for t in range(COMP)] + [own]
            for k in range(NPAR):
                jbuf[z, me, 8 * k : 8 * k + 8] = comp[side, k]
            tile = lane_pack(pack)
            for m in range(1, 4):
                tile = jnp.where(quarter == m, pltpu.roll(tile, J_SPAN * m, 1), tile)
            for m in range(2):
                jbuf[z, me, 16 + m : 17 + m] = jnp.sum(tile[4 * m : 4 * m + 4], axis=0, keepdims=True)
            j_own[...] = own

    def n_copy(side):
        return pltpu.make_async_remote_copy(
            src_ref=n_send.at[side],
            dst_ref=n_recv.at[1 - side],
            send_sem=ns_sem.at[side],
            recv_sem=nr_sem.at[1 - side],
            **to(beside[side]),
        )

    def slot(plane):
        return jbuf.at[plane, me, pl.ds(0, ROWS)]

    def z_copy(plane, peer):
        return pltpu.make_async_remote_copy(
            src_ref=slot(plane), dst_ref=slot(plane), send_sem=zs_sem, recv_sem=zr_sem.at[plane], **to(peer)
        )

    def forward(plane):
        for peer in y_peers:
            pltpu.make_async_remote_copy(
                src_ref=slot(plane), dst_ref=slot(plane), send_sem=ys_sem, recv_sem=yr_sem.at[plane], **to(peer)
            ).start()

    def prepare():
        half_load(1 - pe).wait()

        @pl.when(jnp.logical_not(is_end))
        def _():
            half_load(pe).wait()

        for side in (0, 1):

            @pl.when(interior[side])
            def _():
                end_cells(side)
                source = []
                for t in range(COMP):
                    total = zero
                    for k in range(NPAR):
                        factor = jnp.where(even, coef[side, PE + NPAR * t + k], coef[side, PN + NPAR * t + k])
                        total = total + factor * comp[side, k]
                    source.append(total)
                after = [nxt(v) for v in source]
                for t in range(COMP):
                    total = source[t]
                    for q in range(COMP):
                        total = total + coef[side, DD + COMP * t + q] * source[q]
                        total = total + coef[side, CIN + COMP * t + q] * after[q]
                    src_s[side, t] = source[t]
                    n_send[side, t] = jnp.where(even, source[t], pltpu.roll(coef[side, WT + t] * total, 1, 1))
                n_send[side, COMP] = lane_pack(
                    [coef[side, COUT + i] for i in range(COMP * COMP)] + [coef[side, WT + t] for t in range(COMP)]
                )

    def piece():
        def up(v):
            return jnp.where(lane2 == CELLS - 1, 0.0, pltpu.roll(v, CELLS - 1, 1))

        def down(v):
            return jnp.where(lane2 == 0, 0.0, pltpu.roll(v, 1, 1))

        p_here = [[par[t, k] for k in range(NPAR)] for t in range(COMP)]
        p_up = [[up(v) for v in vs] for vs in p_here]
        p_down = [[down(v) for v in vs] for vs in p_here]

        def product(blocks, cells, start):
            rows = []
            for t in range(COMP):
                row = []
                for k in range(NPAR):
                    total = start[t][k] if start is not None else None
                    for q in range(COMP):
                        term = blocks[t, q] * cells[q][k]
                        total = term if total is None else total + term
                    row.append(total)
                rows.append(row)
            return rows

        b0 = product(diag, p_here, p_here)
        bm = product(left, p_down, None)
        bp = product(right, p_up, None)
        weight = [wt[t] for t in range(COMP)]
        u0 = [[weight[t] * v for v in b0[t]] for t in range(COMP)]
        um = [[weight[t] * v for v in bm[t]] for t in range(COMP)]
        upl = [[weight[t] * v for v in bp[t]] for t in range(COMP)]

        def inner_sum(a, b, k, q):
            total = a[0][k] * b[0][q]
            for t in range(1, COMP):
                total = total + a[t][k] * b[t][q]
            return total

        for k in range(NPAR):
            for q in range(NPAR):
                i = NPAR * k + q
                if k <= q:
                    centre = inner_sum(b0, u0, k, q) + down(inner_sum(bp, upl, k, q)) + up(inner_sum(bm, um, k, q))
                    band[8 + i] = centre
                    if k != q:
                        band[8 + NPAR * q + k] = centre
                one = inner_sum(b0, upl, k, q) + up(inner_sum(bm, u0, k, q))
                two = up(inner_sum(bm, upl, k, q))
                band[12 + i] = one
                band[16 + i] = two
                band[4 + NPAR * q + k] = down(one)
                band[NPAR * q + k] = down(down(two))

        def wide_step(r, carry):
            shifted = []
            for k in range(NPAR):
                a = dirs[0, k, r]
                b = dirs[1, k, r]
                per_offset = []
                for off in (-2, -1, 0, 1, 2):
                    if off == 0:
                        per_offset.append((a, b))
                        continue
                    ra = pltpu.roll(a, -off % LANES, 1)
                    rb = pltpu.roll(b, -off % LANES, 1)
                    if off < 0:
                        per_offset.append((ra, jnp.where(lane < -off, ra, rb)))
                    else:
                        per_offset.append((jnp.where(lane >= LANES - off, rb, ra), rb))
                shifted.append(per_offset)
            for half in (0, 1):
                span = slice(half * LANES, half * LANES + LANES)
                for k in range(NPAR):
                    total = None
                    for o in range(5):
                        for q in range(NPAR):
                            term = band[4 * o + NPAR * k + q, :, span] * shifted[q][o][half]
                            total = term if total is None else total + term
                    hess[k, r, :, span] = total
            return carry

        lax.fori_loop(0, COLS, wide_step, 0, unroll=4)

    @pl.when(early)
    def _():
        prepare()
        piece()

    expected = jnp.where(is_end, 1 + len(z_peers) + len(y_peers), 2)
    pl.semaphore_wait(barrier, expected)

    @pl.when(is_end)
    def _():
        for peer in z_peers:
            z_copy(z, peer).start()
        forward(z)

    @pl.when(jnp.logical_not(early))
    def _():
        prepare()

    for side in (0, 1):

        @pl.when(interior[side])
        def _():
            n_copy(side).start()

    @pl.when(jnp.logical_not(early))
    def _():
        piece()

    def finish(side):
        change = [coef[side, WT + t] * mean_s[side, t] for t in range(COMP)]
        at_end, at_next = [], []
        for q in range(COMP):
            total = change[q] + mean_a[side, q]
            other = zero
            for t in range(COMP):
                total = total + coef[side, DD + COMP * t + q] * change[t]
                other = other + coef[side, CIN + COMP * t + q] * change[t]
            at_end.append(total)
            at_next.append(other)
        corr = []
        for k in range(NPAR):
            c0, c1 = zero, zero
            for t in range(COMP):
                c0 = c0 + coef[side, PE + NPAR * t + k] * at_end[t]
                c1 = c1 + coef[side, PN + NPAR * t + k] * at_next[t]
            straight = jnp.where(even, c0, pltpu.roll(c1, 1, 1))
            corr.append(swap(straight) if side else straight)
        edge = LANES - 2 if side else 0
        here = jnp.logical_and(lane >= edge, lane < edge + 2)
        span = slice(side * LANES, side * LANES + LANES)
        for r in range(COLS):
            for k in range(NPAR):
                moved = pltpu.roll(corr[k], (LANES + edge - 2 * r) % LANES, 1)
                hess[k, r, :, span] = hess[k, r, :, span] + jnp.where(here, moved, 0.0)

    @pl.when(is_end)
    def _():
        for k in reversed(Z_STEPS):
            plane = lax.rem(z + Z_SIZE - k, Z_SIZE)
            z_copy(plane, z_peers[0]).wait_recv()
            forward(plane)

    for side in (0, 1):

        @pl.when(interior[side])
        def _():
            n_copy(1 - side).wait_recv()
            theirs = n_recv[side, COMP]
            out_block = [spread(theirs[:, i : i + 1]) for i in range(COMP * COMP)]
            out_weight = [spread(theirs[:, COMP * COMP + t : COMP * COMP + t + 1]) for t in range(COMP)]
            pairs = [n_recv[side, t] for t in range(COMP)]
            adjoint = []
            for t in range(COMP):
                total, change = zero, zero
                for q in range(COMP):
                    total = total + out_block[COMP * t + q] * src_s[side, q]
                    change = change + coef[side, COUT + COMP * t + q] * pairs[q]
                adjoint.append(nxt(pairs[t]) + out_weight[t] * total)
                mean_s[side, t] = change
            for q in range(COMP):
                total = zero
                for t in range(COMP):
                    total = total + out_block[COMP * t + q] * adjoint[t]
                mean_a[side, q] = total
            finish(side)

    @pl.when(is_end)
    def _():
        own = j_own[...]
        rows = 8 * PIPES

        def arrivals(planes, sem):
            span = jbuf.at[planes, pl.ds(0, 7), pl.ds(0, ROWS)]
            return pltpu.make_async_remote_copy(
                src_ref=span, dst_ref=span, send_sem=ys_sem, recv_sem=yr_sem.at[sem], **to(y_peers[0])
            )

        j_sum[...] = jnp.zeros_like(j_sum)
        j_weight[...] = jnp.zeros_like(j_weight)
        degree = zero
        for end in (0, 1):
            for half in (0, 1):
                row = ids[end, :, half * LANES : half * LANES + LANES].astype(F32)
                degree = degree + jnp.where(row == own, 1.0, 0.0)
        share = 1.0 / spread(jnp.sum(degree, axis=1, keepdims=True))

        def add_planes(j, carry):
            pair = [lax.rem(z + Z_SIZE - j, Z_SIZE), lax.rem(z + 1 + j, Z_SIZE)]
            columns, tiles = [], []
            for plane in pair:
                arrivals(plane, plane).wait_recv()
                columns.append([jbuf[plane, :, 8 * k : 8 * k + 8].reshape(rows, LANES) for k in range(NPAR)])
                for q in range(8):
                    packed = jnp.where(
                        iota((PIPES, LANES), 0) < 4, jbuf[plane, q, 16:17], jbuf[plane, q, 17:18]
                    )
                    tile = packed
                    for m in range(1, 4):
                        tile = jnp.where(quarter == m, pltpu.roll(packed, LANES - J_SPAN * m, 1), tile)
                    tiles.append(tile)
            x_parts = split(jnp.concatenate([jnp.concatenate(c, axis=1) for c in columns]))
            coefs = jnp.concatenate(tiles).T
            same = coefs[J_ID : J_ID + 1] == own[:, 0:1]
            w_parts = [
                jnp.concatenate([jnp.where(same, v[i : i + 1], 0.0) for i in range(J_W)]).astype(BF16)
                for v in split(coefs[:J_SPAN], F32)
            ]
            order = ((0, 0), (0, 1), (1, 0), (0, 2), (2, 0), (1, 1))
            j_sum[...] += jnp.dot(
                jnp.concatenate([w_parts[i] for i, _ in order], axis=1),
                jnp.concatenate([x_parts[i] for _, i in order]),
                preferred_element_type=F32,
            )
            for t in range(COMP):
                j_weight[t] += jnp.where(same, coefs[J_W + t : J_W + t + 1], 0.0)
            return carry

        lax.fori_loop(0, Z_SIZE // 2, add_planes, 0)

        def part(c, k):
            return j_sum[PIPES * c : PIPES * c + PIPES, LANES * k : LANES * k + LANES]

        for t in range(COMP):
            c = NPAR * t
            mean = share * (part(c, 0) + part(c + 1, 1))
            near = part(8 + c, 0) + part(9 + c, 1)
            far = part(16 + c, 0) + part(17 + c, 1)
            weights = spread(jnp.sum(j_weight[t], axis=1, keepdims=True))
            mean_s[pe, t] = 0.5 * mean
            mean_a[pe, t] = 0.5 * share * (near + nxt(far) + 0.5 * weights * mean)
        for side, chosen in ((0, is_first), (1, is_last)):

            @pl.when(chosen)
            def _():
                finish(side)

        arrivals(slice(None), 0).wait_send()
        span = jbuf.at[0, pl.ds(0, 7), pl.ds(0, ROWS)]
        pltpu.make_async_remote_copy(
            src_ref=span, dst_ref=span, send_sem=zs_sem, recv_sem=yr_sem.at[0], **to(z_peers[0])
        ).wait_send()

    for side in (0, 1):

        @pl.when(interior[side])
        def _():
            n_copy(side).wait_send()


def on_device(directions, diag_blocks, left_blocks, right_blocks, param_blocks, obs_weight, end_junction):
    args = (directions, diag_blocks, left_blocks, right_blocks, param_blocks, obs_weight, jnp.swapaxes(end_junction, 1, 2))
    args = tuple(pltpu.with_memory_space_constraint(a, pltpu.HBM) for a in args)
    dma = pltpu.SemaphoreType.DMA

    def tiles(*counts):
        return pltpu.VMEM(counts + (PIPES, LANES), F32)

    return pl.pallas_call(
        kernel,
        out_shape=pltpu.VMEM(directions.shape, F32),
        in_specs=[pl.BlockSpec(memory_space=pl.ANY)] * len(args),
        out_specs=pl.BlockSpec(memory_space=pltpu.VMEM),
        scratch_shapes=[tiles(2, NPAR, COLS)]
        + [pltpu.VMEM(a.shape, a.dtype) for a in args[1:]]
        + [
            pltpu.VMEM((5 * NPAR * NPAR, PIPES, CELLS), F32),
            tiles(2, N_COEF),
            tiles(2, NPAR),
            tiles(2, COMP),
            tiles(2, COMP + 1),
            tiles(2, COMP + 1),
            pltpu.VMEM((Z_SIZE, 8, 24, LANES), F32),
            pltpu.VMEM((PIPES * J_W, 2 * LANES), F32),
            tiles(COMP),
            tiles(),
            tiles(2, COMP),
            tiles(2, COMP),
            dma((2,)),
            dma((6,)),
            dma((2,)),
            dma((2,)),
            dma,
            dma((8,)),
            dma,
            dma((8,)),
        ],
        compiler_params=pltpu.CompilerParams(
            collective_id=3, has_side_effects=True, vmem_limit_bytes=56 * 1024 * 1024
        ),
    )(*args)


def solution(mesh):
    return jax.shard_map(
        on_device,
        mesh=mesh,
        in_specs=(
            P(None, None, "region", "sub"),
            P(None, None, "region", "sub"),
            P(None, None, "region", "sub"),
            P(None, None, "region", "sub"),
            P(None, None, "region", "sub"),
            P(None, "region", "sub"),
            P(),
        ),
        out_specs=P(None, None, "region", "sub"),
        check_vma=False,
    )
```

time: 21.1 us -> 19.4 us (0.919)
  Pallas kernels: 20 us -> 18.4 us
    pallas_call x1, Pallas kernels: 20 us -> 18.4 us  [on_device(): pl.pallas_call(kernel, out_shape=pltpu.VMEM(directions.shape, F32), in_sp...]
where the time goes in v3:
time: 19.4 us; the launch traced here: 19.3 us
  Pallas kernels  18.4 us (95%)
  local copies, waits for them, and re-layouts  0.97 us (5%)
    pallas_call x1, Pallas kernels, on_device(): pl.pallas_call(kernel, out_shape=pltpu.VMEM(directions.shape, F32), in_sp...  18.4 us
    unnamed x1, local copies, waits for them, and re-layouts  0.97 us

profile of v3, /device:TPU:32, one launch (start us, length us, event | category | flops | bytes accessed | tf_op | source)
XLA Modules:
  0.0 19.3 jit_solution(9050059998058635124)
XLA Ops:
  0.0 18.4 %shard_map.73 = f32[2,64,8,256]{3,2,1,0:T(8,128)S(1)} custom-call(f32[2,64,8,256]{3,2,1,0:T(8,128)} %dir_in.1, f32[4,4,8,256]{3,2,1,0:T(8,128)} %diag_in.1, f32[4,4,8,256]{3,2,1,0:T(8,128)} %left_in.1, f32[4,4,8,256]{3,2,1,0:T(8,128)} %right_in.1, f32[4,2,8,256]{3,2,1,0:T(8,128)} %par_in.1, f32[4,8,256]{2,1,0:T(8,128)} %wt_in.1, s32[2,1,256]{2,1,0:T(1,128)} %bitcast.1), custom_call_target="tpu_custom_call" | custom-call | tf_op jit(solution)/shard_map/pallas_call | solution.py:487
  18.4 1.0 %copy.9 = f32[2,64,8,256]{3,2,1,0:T(8,128)} copy(f32[2,64,8,256]{3,2,1,0:T(8,128)S(1)} %shard_map.73) | data formatting | bytes 2097152

commit v4 on v3

--- a/solution.py
+++ b/solution.py
@@ -12,6 +12,7 @@
 COMP, NPAR, COLS, PIPES, CELLS = 4, 2, 64, 8, 256
 LANES = 128
 Z_STEPS = (4, 3, 5, 2, 6, 1, 7)
+DIRECT = ((4, 0),)
 PE, PN, DD, CIN, COUT, WT = 0, 8, 16, 32, 48, 64
 N_COEF = 68
 J_W, J_ID, J_SPAN = 24, 28, 32
@@ -51,8 +52,12 @@
     pe = s // 7
 
     z_peers = [(x * Z_SIZE + lax.rem(z + k, Z_SIZE), s) for k in Z_STEPS]
-    xr = [lax.rem(x + k, X_SIZE) * Z_SIZE + z for k in range(X_SIZE)]
-    y_peers = [(xr[2], 7 - s), (xr[1], 7 - s), (xr[3], 7 - s), (xr[2], s), (xr[1], s), (xr[3], s), (g, 7 - s)]
+
+    def plane_peers(plane):
+        xr = [lax.rem(x + k, X_SIZE) * Z_SIZE + plane for k in range(X_SIZE)]
+        return [(xr[2], 7 - s), (xr[1], 7 - s), (xr[3], 7 - s), (xr[2], s), (xr[1], s), (xr[3], s), (xr[0], 7 - s)]
+
+    y_peers = plane_peers(z)
 
     def to(peer):
         return dict(device_id={"region": peer[0], "sub": peer[1]}, device_id_type=MESH)
@@ -70,12 +75,21 @@
             ((par_in, par), (diag_in, diag), (wt_in, wt), (left_in, left), (right_in, right), (ids_in, ids))
         )
     ]
+    half_load(pe).start()
+    for load in loads:
+        load.start()
     barrier = pltpu.get_barrier_semaphore()
 
     @pl.when(is_end)
     def _():
         for peer in z_peers + y_peers:
             pl.semaphore_signal(barrier, inc=1, **to(peer))
+        for source, target in DIRECT:
+
+            @pl.when(z == target)
+            def _():
+                for peer in plane_peers(source):
+                    pl.semaphore_signal(barrier, inc=1, **to(peer))
 
     for side in (0, 1):
 
@@ -83,9 +97,6 @@
         def _():
             pl.semaphore_signal(barrier, inc=1, **to(beside[side]))
 
-    half_load(pe).start()
-    for load in loads:
-        load.start()
     half_load(1 - pe).start()
     for load in loads:
         load.wait()
@@ -115,18 +126,17 @@
         return tile
 
     def end_cells(side):
-        def step(j, tiles):
-            tiles = list(tiles)
-            for u in range(4):
-                r = j * 4 + u
-                shift = lax.rem(2 * r + 2 * side, LANES)
-                for k in range(NPAR):
-                    tiles[k] = jnp.where(lane // 2 == r, pltpu.roll(dirs[side, k, r], shift, 1), tiles[k])
-            return tuple(tiles)
-
-        tiles = lax.fori_loop(0, COLS // 4, step, (zero,) * NPAR, unroll=4)
+        parts = [[zero, zero] for _ in range(NPAR)]
+        for r in range(COLS):
+            here = lane // 2 == r
+            for k in range(NPAR):
+                moved = pltpu.roll(dirs[side, k, r], (2 * r + 2 * side) % LANES, 1)
+                parts[k][r % 2] = jnp.where(here, moved, parts[k][r % 2])
+        tiles = [a + b for a, b in parts]
         for k in range(NPAR):
             comp[side, k] = swap(tiles[k]) if side else tiles[k]
+
+    def end_coefficients(side, outside):
         e, n = (CELLS - 1, CELLS - 2) if side else (0, 1)
         inner, outer = (left, right) if side else (right, left)
         for t in range(COMP):
@@ -137,33 +147,38 @@
             for q in range(COMP):
                 coef[side, DD + COMP * t + q] = spread(diag[t, q, :, e : e + 1])
                 coef[side, CIN + COMP * t + q] = spread(inner[t, q, :, e : e + 1])
-                coef[side, COUT + COMP * t + q] = spread(outer[t, q, :, e : e + 1])
-
-    @pl.when(is_end)
-    def _():
-        half_load(pe).wait()
+                if outside:
+                    coef[side, COUT + COMP * t + q] = spread(outer[t, q, :, e : e + 1])
 
     for side, chosen in ((0, is_first), (1, is_last)):
 
         @pl.when(chosen)
         def _():
-            end_cells(side)
             row = jnp.where(g >= 16, ids[side, :, LANES:], ids[side, :, :LANES]).astype(F32)
             mine = lane == PIPES * lax.rem(g, 16) + iota((PIPES, LANES), 0)
             own = spread(jnp.sum(jnp.where(mine, row, 0.0), axis=1, keepdims=True))
-            pack = [coef[side, PE + i] for i in range(COMP * NPAR)]
+            span = slice(side * LANES, side * LANES + LANES)
+            inner = left if side else right
+            here = [[par[t, k, :, span] for k in range(NPAR)] for t in range(COMP)]
+            beyond = [[pltpu.roll(v, 1 if side else LANES - 1, 1) for v in vs] for vs in here]
+            weight = [wt[t, :, span] for t in range(COMP)]
+            pack = [v for vs in here for v in vs]
             for near in (True, False):
                 for t in range(COMP):
                     for k in range(NPAR):
-                        total = coef[side, PE + NPAR * t + k] if near else zero
+                        total = here[t][k] if near else zero
                         for q in range(COMP):
-                            block, cell = (DD, PE) if near else (CIN, PN)
-                            total = total + coef[side, block + COMP * t + q] * coef[side, cell + NPAR * q + k]
-                        pack.append(coef[side, WT + t] * total)
-            pack += [coef[side, WT + t] for t in range(COMP)] + [own]
+                            block, cell = (diag, here) if near else (inner, beyond)
+                            total = total + block[t, q, :, span] * cell[q][k]
+                        pack.append(weight[t] * total)
+            pack += weight
+            tile = jnp.where(lane == J_ID, own, 0.0)
+            for i, v in enumerate(pack):
+                tile = jnp.where(lane == i, pltpu.roll(v, (i - (LANES - 1) * side) % LANES, 1), tile)
+            half_load(pe).wait()
+            end_cells(side)
             for k in range(NPAR):
                 jbuf[z, me, 8 * k : 8 * k + 8] = comp[side, k]
-            tile = lane_pack(pack)
             for m in range(1, 4):
                 tile = jnp.where(quarter == m, pltpu.roll(tile, J_SPAN * m, 1), tile)
             for m in range(2):
@@ -187,8 +202,8 @@
             src_ref=slot(plane), dst_ref=slot(plane), send_sem=zs_sem, recv_sem=zr_sem.at[plane], **to(peer)
         )
 
-    def forward(plane):
-        for peer in y_peers:
+    def forward(plane, peers=y_peers):
+        for peer in peers:
             pltpu.make_async_remote_copy(
                 src_ref=slot(plane), dst_ref=slot(plane), send_sem=ys_sem, recv_sem=yr_sem.at[plane], **to(peer)
             ).start()
@@ -205,6 +220,7 @@
             @pl.when(interior[side])
             def _():
                 end_cells(side)
+                end_coefficients(side, True)
                 source = []
                 for t in range(COMP):
                     total = zero
@@ -223,6 +239,12 @@
                 n_send[side, COMP] = lane_pack(
                     [coef[side, COUT + i] for i in range(COMP * COMP)] + [coef[side, WT + t] for t in range(COMP)]
                 )
+
+        for side, chosen in ((0, is_first), (1, is_last)):
+
+            @pl.when(chosen)
+            def _():
+                end_coefficients(side, False)
 
     def piece():
         def up(v):
@@ -313,12 +335,25 @@
         piece()
 
     expected = jnp.where(is_end, 1 + len(z_peers) + len(y_peers), 2)
+    for source, _ in DIRECT:
+        expected = expected + jnp.where(jnp.logical_and(is_end, z == source), len(y_peers), 0)
     pl.semaphore_wait(barrier, expected)
 
     @pl.when(is_end)
     def _():
-        for peer in z_peers:
-            z_copy(z, peer).start()
+        for plane in range(Z_SIZE):
+
+            @pl.when(z != plane)
+            def _():
+                z_copy(z, (x * Z_SIZE + plane, s)).start()
+
+            for source, target in DIRECT:
+                if target == plane:
+
+                    @pl.when(z == source)
+                    def _():
+                        forward(z, plane_peers(target))
+
         forward(z)
 
     @pl.when(jnp.logical_not(early))
@@ -367,7 +402,14 @@
         for k in reversed(Z_STEPS):
             plane = lax.rem(z + Z_SIZE - k, Z_SIZE)
             z_copy(plane, z_peers[0]).wait_recv()
-            forward(plane)
+            sent = z < 0
+            for source, target in DIRECT:
+                sent = jnp.logical_or(sent, jnp.logical_and(z == target, plane == source))
+
+            @pl.when(jnp.logical_not(sent))
+            def _():
+                forward(plane)
+
 
     for side in (0, 1):
 
@@ -463,7 +505,22 @@
             def _():
                 finish(side)
 
-        arrivals(slice(None), 0).wait_send()
+        for plane in range(Z_SIZE):
+            sent = z < 0
+            for source, target in DIRECT:
+                if source == plane:
+                    sent = jnp.logical_or(sent, z == target)
+
+            @pl.when(jnp.logical_not(sent))
+            def _():
+                arrivals(plane, plane).wait_send()
+
+        for source, target in DIRECT:
+
+            @pl.when(z == source)
+            def _():
+                arrivals(target, target).wait_send()
+
         span = jbuf.at[0, pl.ds(0, 7), pl.ds(0, ROWS)]
         pltpu.make_async_remote_copy(
             src_ref=span, dst_ref=span, send_sem=zs_sem, recv_sem=yr_sem.at[0], **to(z_peers[0])

time: 19.4 us -> 18.9 us (0.974)
  Pallas kernels: 18.4 us -> 17.8 us
    pallas_call x1, Pallas kernels: 18.4 us -> 17.8 us  [on_device(): pl.pallas_call(kernel, out_shape=pltpu.VMEM(directions.shape, F32), in_sp...]
where the time goes in v4:
time: 18.9 us; the launch traced here: 18.8 us
  Pallas kernels  17.8 us (94%)
  local copies, waits for them, and re-layouts  0.97 us (5%)
    pallas_call x1, Pallas kernels, on_device(): pl.pallas_call(kernel, out_shape=pltpu.VMEM(directions.shape, F32), in_sp...  17.8 us
    unnamed x1, local copies, waits for them, and re-layouts  0.97 us

profile of v4, /device:TPU:32, one launch (start us, length us, event | category | flops | bytes accessed | tf_op | source)
XLA Modules:
  0.0 18.8 jit_solution(10637654588299941702)
XLA Ops:
  0.0 17.8 %shard_map.73 = f32[2,64,8,256]{3,2,1,0:T(8,128)S(1)} custom-call(f32[2,64,8,256]{3,2,1,0:T(8,128)} %dir_in.1, f32[4,4,8,256]{3,2,1,0:T(8,128)} %diag_in.1, f32[4,4,8,256]{3,2,1,0:T(8,128)} %left_in.1, f32[4,4,8,256]{3,2,1,0:T(8,128)} %right_in.1, f32[4,2,8,256]{3,2,1,0:T(8,128)} %par_in.1, f32[4,8,256]{2,1,0:T(8,128)} %wt_in.1, s32[2,1,256]{2,1,0:T(1,128)} %bitcast.1), custom_call_target="tpu_custom_call" | custom-call | tf_op jit(solution)/shard_map/pallas_call | solution.py:544
  17.8 1.0 %copy.9 = f32[2,64,8,256]{3,2,1,0:T(8,128)} copy(f32[2,64,8,256]{3,2,1,0:T(8,128)S(1)} %shard_map.73) | data formatting | bytes 2097152

commit v5 on v4

--- a/solution.py
+++ b/solution.py
@@ -37,7 +37,7 @@
 
 
 def kernel(
-    dir_in, diag_in, left_in, right_in, par_in, wt_in, ids_in, hess,
+    dir_in, diag_in, left_in, right_in, par_in, wt_in, ids_in, hess, last,
     dirs, diag, left, right, par, wt, ids,
     band, coef, comp, src_s, n_send, n_recv, jbuf, j_sum, j_weight, j_own, mean_s, mean_a,
     dir_sem, in_sem, ns_sem, nr_sem, zs_sem, zr_sem, ys_sem, yr_sem,
@@ -389,6 +389,9 @@
                 c1 = c1 + coef[side, PN + NPAR * t + k] * at_next[t]
             straight = jnp.where(even, c0, pltpu.roll(c1, 1, 1))
             corr.append(swap(straight) if side else straight)
+        return corr
+
+    def add_to_piece(side, corr):
         edge = LANES - 2 if side else 0
         here = jnp.logical_and(lane >= edge, lane < edge + 2)
         span = slice(side * LANES, side * LANES + LANES)
@@ -433,7 +436,7 @@
                 for t in range(COMP):
                     total = total + out_block[COMP * t + q] * adjoint[t]
                 mean_a[side, q] = total
-            finish(side)
+            add_to_piece(side, finish(side))
 
     @pl.when(is_end)
     def _():
@@ -503,7 +506,8 @@
 
             @pl.when(chosen)
             def _():
-                finish(side)
+                for k, v in enumerate(finish(side)):
+                    last[k] = v
 
         for plane in range(Z_SIZE):
             sent = z < 0
@@ -533,6 +537,39 @@
             n_copy(side).wait_send()
 
 
+def write_kernel(hess, last, out, piece, sem):
+    s = lax.axis_index("sub")
+    lane = iota((PIPES, LANES), 1)
+
+    def write(side, k, source):
+        span = pl.ds(side * LANES, LANES)
+        return pltpu.make_async_copy(source, out.at[k, :, :, span], sem.at[side, k])
+
+    for side in (0, 1):
+
+        @pl.when(s != 7 * side)
+        def _():
+            for k in range(NPAR):
+                write(side, k, hess.at[k, :, :, pl.ds(side * LANES, LANES)]).start()
+
+    for side in (0, 1):
+
+        @pl.when(s == 7 * side)
+        def _():
+            edge = LANES - 2 if side else 0
+            here = jnp.logical_and(lane >= edge, lane < edge + 2)
+            for k in range(NPAR):
+                corr = last[k]
+                for r in range(COLS):
+                    moved = pltpu.roll(corr, (LANES + edge - 2 * r) % LANES, 1)
+                    piece[k, r] = hess[k, r, :, side * LANES : side * LANES + LANES] + jnp.where(here, moved, 0.0)
+                write(side, k, piece.at[k]).start()
+
+    for side in (0, 1):
+        for k in range(NPAR):
+            write(side, k, piece.at[k]).wait()
+
+
 def on_device(directions, diag_blocks, left_blocks, right_blocks, param_blocks, obs_weight, end_junction):
     args = (directions, diag_blocks, left_blocks, right_blocks, param_blocks, obs_weight, jnp.swapaxes(end_junction, 1, 2))
     args = tuple(pltpu.with_memory_space_constraint(a, pltpu.HBM) for a in args)
@@ -541,11 +578,11 @@
     def tiles(*counts):
         return pltpu.VMEM(counts + (PIPES, LANES), F32)
 
-    return pl.pallas_call(
+    hess, last = pl.pallas_call(
         kernel,
-        out_shape=pltpu.VMEM(directions.shape, F32),
+        out_shape=(pltpu.VMEM(directions.shape, F32), tiles(NPAR)),
         in_specs=[pl.BlockSpec(memory_space=pl.ANY)] * len(args),
-        out_specs=pl.BlockSpec(memory_space=pltpu.VMEM),
+        out_specs=[pl.BlockSpec(memory_space=pltpu.VMEM)] * 2,
         scratch_shapes=[tiles(2, NPAR, COLS)]
         + [pltpu.VMEM(a.shape, a.dtype) for a in args[1:]]
         + [
@@ -574,6 +611,13 @@
             collective_id=3, has_side_effects=True, vmem_limit_bytes=56 * 1024 * 1024
         ),
     )(*args)
+    return pl.pallas_call(
+        write_kernel,
+        out_shape=jax.ShapeDtypeStruct(directions.shape, F32),
+        in_specs=[pl.BlockSpec(memory_space=pltpu.VMEM)] * 2,
+        out_specs=pl.BlockSpec(memory_space=pl.ANY),
+        scratch_shapes=[tiles(NPAR, COLS), dma((2, NPAR))],
+    )(*(pltpu.with_memory_space_constraint(v, pltpu.VMEM) for v in (hess, last)))
 
 
 def solution(mesh):

time: 18.9 us -> 18.7 us (0.989)
  local copies, waits for them, and re-layouts: 0.97 us -> 0 us
  Pallas kernels: 17.8 us -> 18.6 us
    unnamed x1 -> x0, local copies, waits for them, and re-layouts: 0.97 us -> none
    pallas_call x1 -> x2, Pallas kernels: 17.8 us -> 18.6 us  [the longest x1 17.6 us: on_device(): pl.pallas_call(kernel, out_shape=(pltpu.VMEM(directions.shape, F32), tile...]
where the time goes in v5:
time: 18.7 us; the launch traced here: 18.6 us
  Pallas kernels  18.6 us (99%)
    pallas_call x1, Pallas kernels, on_device(): pl.pallas_call(kernel, out_shape=(pltpu.VMEM(directions.shape, F32), tile...  17.6 us
    pallas_call x1, Pallas kernels, on_device(): pl.pallas_call(write_kernel, out_shape=jax.ShapeDtypeStruct(directions.sh...  1.01 us

profile of v5, /device:TPU:32, one launch (start us, length us, event | category | flops | bytes accessed | tf_op | source)
XLA Modules:
  0.0 18.6 jit_solution(16881062425506422593)
XLA Ops:
  0.0 17.6 %shard_map.73 = (f32[2,64,8,256]{3,2,1,0:T(8,128)S(1)}, f32[2,8,128]{2,1,0:T(8,128)S(1)}) custom-call(f32[2,64,8,256]{3,2,1,0:T(8,128)} %dir_in.1, f32[4,4,8,256]{3,2,1,0:T(8,128)} %diag_in.1, f32[4,4,8,256]{3,2,1,0:T(8,128)} %left_in.1, f32[4,4,8,256]{3,2,1,0:T(8,128)} %right_in.1, f32[4,2,8,256]{3,2,1,0:T(8,128)} %par_in.1, f32[4,8,256]{2,1,0:T(8,128)} %wt_in.1, ...), custom_call_target="tpu_custom_call" | custom-call | tf_op jit(solution)/shard_map/pallas_call | solution.py:581
  17.6 1.0 %shard_map.74 = f32[2,64,8,256]{3,2,1,0:T(8,128)} custom-call(f32[2,64,8,256]{3,2,1,0:T(8,128)S(1)} %get-tuple-element.7.hess, f32[2,8,128]{2,1,0:T(8,128)S(1)} %get-tuple-element.8.last), custom_call_target="tpu_custom_call" | custom-call | tf_op jit(solution)/shard_map/pallas_call | solution.py:614

commit v6 on v5

--- a/solution.py
+++ b/solution.py
@@ -194,6 +194,15 @@
             **to(beside[side]),
         )
 
+    def n_arrival(side):
+        return pltpu.make_async_remote_copy(
+            src_ref=n_send.at[side],
+            dst_ref=n_recv.at[side],
+            send_sem=ns_sem.at[side],
+            recv_sem=nr_sem.at[side],
+            **to(beside[side]),
+        )
+
     def slot(plane):
         return jbuf.at[plane, me, pl.ds(0, ROWS)]
 
@@ -418,7 +427,7 @@
 
         @pl.when(interior[side])
         def _():
-            n_copy(1 - side).wait_recv()
+            n_arrival(side).wait_recv()
             theirs = n_recv[side, COMP]
             out_block = [spread(theirs[:, i : i + 1]) for i in range(COMP * COMP)]
             out_weight = [spread(theirs[:, COMP * COMP + t : COMP * COMP + t + 1]) for t in range(COMP)]
@@ -463,7 +472,8 @@
             columns, tiles = [], []
             for plane in pair:
                 arrivals(plane, plane).wait_recv()
-                columns.append([jbuf[plane, :, 8 * k : 8 * k + 8].reshape(rows, LANES) for k in range(NPAR)])
+                halves = [jbuf[plane, :, 8 * k : 8 * k + 8].reshape(rows, LANES) for k in range(NPAR)]
+                columns.append(split(jnp.concatenate(halves, axis=1)))
                 for q in range(8):
                     packed = jnp.where(
                         iota((PIPES, LANES), 0) < 4, jbuf[plane, q, 16:17], jbuf[plane, q, 17:18]
@@ -472,7 +482,7 @@
                     for m in range(1, 4):
                         tile = jnp.where(quarter == m, pltpu.roll(packed, LANES - J_SPAN * m, 1), tile)
                     tiles.append(tile)
-            x_parts = split(jnp.concatenate([jnp.concatenate(c, axis=1) for c in columns]))
+            x_parts = [jnp.concatenate([c[i] for c in columns]) for i in range(3)]
             coefs = jnp.concatenate(tiles).T
             same = coefs[J_ID : J_ID + 1] == own[:, 0:1]
             w_parts = [

time: 18.7 us -> 18.7 us (level)
  no operation moved by 1% of the time
where the time goes in v6:
time: 18.7 us; the launch traced here: 18.6 us
  Pallas kernels  18.6 us (99%)
    pallas_call x1, Pallas kernels, on_device(): pl.pallas_call(kernel, out_shape=(pltpu.VMEM(directions.shape, F32), tile...  17.6 us
    pallas_call x1, Pallas kernels, on_device(): pl.pallas_call(write_kernel, out_shape=jax.ShapeDtypeStruct(directions.sh...  1.01 us

profile of v6, /device:TPU:32, one launch (start us, length us, event | category | flops | bytes accessed | tf_op | source)
XLA Modules:
  0.0 18.6 jit_solution(1135184680615783118)
XLA Ops:
  0.0 17.6 %shard_map.73 = (f32[2,64,8,256]{3,2,1,0:T(8,128)S(1)}, f32[2,8,128]{2,1,0:T(8,128)S(1)}) custom-call(f32[2,64,8,256]{3,2,1,0:T(8,128)} %dir_in.1, f32[4,4,8,256]{3,2,1,0:T(8,128)} %diag_in.1, f32[4,4,8,256]{3,2,1,0:T(8,128)} %left_in.1, f32[4,4,8,256]{3,2,1,0:T(8,128)} %right_in.1, f32[4,2,8,256]{3,2,1,0:T(8,128)} %par_in.1, f32[4,8,256]{2,1,0:T(8,128)} %wt_in.1, ...), custom_call_target="tpu_custom_call" | custom-call | tf_op jit(solution)/shard_map/pallas_call | solution.py:591
  17.6 1.0 %shard_map.74 = f32[2,64,8,256]{3,2,1,0:T(8,128)} custom-call(f32[2,64,8,256]{3,2,1,0:T(8,128)S(1)} %get-tuple-element.7.hess, f32[2,8,128]{2,1,0:T(8,128)S(1)} %get-tuple-element.8.last), custom_call_target="tpu_custom_call" | custom-call | tf_op jit(solution)/shard_map/pallas_call | solution.py:624

commit v7 on v6

--- a/solution.py
+++ b/solution.py
@@ -12,7 +12,7 @@
 COMP, NPAR, COLS, PIPES, CELLS = 4, 2, 64, 8, 256
 LANES = 128
 Z_STEPS = (4, 3, 5, 2, 6, 1, 7)
-DIRECT = ((4, 0),)
+DIRECT = ((4, 0), (3, 0), (5, 1))
 PE, PN, DD, CIN, COUT, WT = 0, 8, 16, 32, 48, 64
 N_COEF = 68
 J_W, J_ID, J_SPAN = 24, 28, 32
@@ -211,6 +211,12 @@
             src_ref=slot(plane), dst_ref=slot(plane), send_sem=zs_sem, recv_sem=zr_sem.at[plane], **to(peer)
         )
 
+    def went_straight(plane):
+        answer = z < 0
+        for source, target in DIRECT:
+            answer = jnp.logical_or(answer, jnp.logical_and(z == target, plane == source))
+        return answer
+
     def forward(plane, peers=y_peers):
         for peer in peers:
             pltpu.make_async_remote_copy(
@@ -356,12 +362,11 @@
             def _():
                 z_copy(z, (x * Z_SIZE + plane, s)).start()
 
-            for source, target in DIRECT:
-                if target == plane:
-
-                    @pl.when(z == source)
-                    def _():
-                        forward(z, plane_peers(target))
+        for source, target in DIRECT:
+
+            @pl.when(z == source)
+            def _():
+                forward(z, plane_peers(target))
 
         forward(z)
 
@@ -409,43 +414,45 @@
                 moved = pltpu.roll(corr[k], (LANES + edge - 2 * r) % LANES, 1)
                 hess[k, r, :, span] = hess[k, r, :, span] + jnp.where(here, moved, 0.0)
 
+    def beside_part():
+        for side in (0, 1):
+
+            @pl.when(interior[side])
+            def _():
+                n_arrival(side).wait_recv()
+                theirs = n_recv[side, COMP]
+                out_block = [spread(theirs[:, i : i + 1]) for i in range(COMP * COMP)]
+                out_weight = [spread(theirs[:, COMP * COMP + t : COMP * COMP + t + 1]) for t in range(COMP)]
+                pairs = [n_recv[side, t] for t in range(COMP)]
+                adjoint = []
+                for t in range(COMP):
+                    total, change = zero, zero
+                    for q in range(COMP):
+                        total = total + out_block[COMP * t + q] * src_s[side, q]
+                        change = change + coef[side, COUT + COMP * t + q] * pairs[q]
+                    adjoint.append(nxt(pairs[t]) + out_weight[t] * total)
+                    mean_s[side, t] = change
+                for q in range(COMP):
+                    total = zero
+                    for t in range(COMP):
+                        total = total + out_block[COMP * t + q] * adjoint[t]
+                    mean_a[side, q] = total
+                add_to_piece(side, finish(side))
+
+    pl.when(early)(beside_part)
+
     @pl.when(is_end)
     def _():
         for k in reversed(Z_STEPS):
             plane = lax.rem(z + Z_SIZE - k, Z_SIZE)
-            z_copy(plane, z_peers[0]).wait_recv()
-            sent = z < 0
-            for source, target in DIRECT:
-                sent = jnp.logical_or(sent, jnp.logical_and(z == target, plane == source))
-
-            @pl.when(jnp.logical_not(sent))
-            def _():
+
+            @pl.when(jnp.logical_not(went_straight(plane)))
+            def _():
+                z_copy(plane, z_peers[0]).wait_recv()
                 forward(plane)
 
 
-    for side in (0, 1):
-
-        @pl.when(interior[side])
-        def _():
-            n_arrival(side).wait_recv()
-            theirs = n_recv[side, COMP]
-            out_block = [spread(theirs[:, i : i + 1]) for i in range(COMP * COMP)]
-            out_weight = [spread(theirs[:, COMP * COMP + t : COMP * COMP + t + 1]) for t in range(COMP)]
-            pairs = [n_recv[side, t] for t in range(COMP)]
-            adjoint = []
-            for t in range(COMP):
-                total, change = zero, zero
-                for q in range(COMP):
-                    total = total + out_block[COMP * t + q] * src_s[side, q]
-                    change = change + coef[side, COUT + COMP * t + q] * pairs[q]
-                adjoint.append(nxt(pairs[t]) + out_weight[t] * total)
-                mean_s[side, t] = change
-            for q in range(COMP):
-                total = zero
-                for t in range(COMP):
-                    total = total + out_block[COMP * t + q] * adjoint[t]
-                mean_a[side, q] = total
-            add_to_piece(side, finish(side))
+    pl.when(jnp.logical_not(early))(beside_part)
 
     @pl.when(is_end)
     def _():
@@ -472,6 +479,11 @@
             columns, tiles = [], []
             for plane in pair:
                 arrivals(plane, plane).wait_recv()
+
+                @pl.when(went_straight(plane))
+                def _():
+                    z_copy(plane, z_peers[0]).wait_recv()
+
                 halves = [jbuf[plane, :, 8 * k : 8 * k + 8].reshape(rows, LANES) for k in range(NPAR)]
                 columns.append(split(jnp.concatenate(halves, axis=1)))
                 for q in range(8):

time: 18.7 us -> 18.5 us (0.989)
  Pallas kernels: 18.6 us -> 18.3 us
    pallas_call x1, Pallas kernels: 17.6 us -> 17.3 us  [on_device(): pl.pallas_call(kernel, out_shape=(pltpu.VMEM(directions.shape, F32), tile...]
where the time goes in v7:
time: 18.5 us; the launch traced here: 18.3 us
  Pallas kernels  18.3 us (99%)
    pallas_call x1, Pallas kernels, on_device(): pl.pallas_call(kernel, out_shape=(pltpu.VMEM(directions.shape, F32), tile...  17.3 us
    pallas_call x1, Pallas kernels, on_device(): pl.pallas_call(write_kernel, out_shape=jax.ShapeDtypeStruct(directions.sh...  1.01 us

profile of v7, /device:TPU:32, one launch (start us, length us, event | category | flops | bytes accessed | tf_op | source)
XLA Modules:
  0.0 18.3 jit_solution(11905079179493041594)
XLA Ops:
  0.0 17.3 %shard_map.73 = (f32[2,64,8,256]{3,2,1,0:T(8,128)S(1)}, f32[2,8,128]{2,1,0:T(8,128)S(1)}) custom-call(f32[2,64,8,256]{3,2,1,0:T(8,128)} %dir_in.1, f32[4,4,8,256]{3,2,1,0:T(8,128)} %diag_in.1, f32[4,4,8,256]{3,2,1,0:T(8,128)} %left_in.1, f32[4,4,8,256]{3,2,1,0:T(8,128)} %right_in.1, f32[4,2,8,256]{3,2,1,0:T(8,128)} %par_in.1, f32[4,8,256]{2,1,0:T(8,128)} %wt_in.1, ...), custom_call_target="tpu_custom_call" | custom-call | tf_op jit(solution)/shard_map/pallas_call | solution.py:603
  17.3 1.0 %shard_map.74 = f32[2,64,8,256]{3,2,1,0:T(8,128)} custom-call(f32[2,64,8,256]{3,2,1,0:T(8,128)S(1)} %get-tuple-element.7.hess, f32[2,8,128]{2,1,0:T(8,128)S(1)} %get-tuple-element.8.last), custom_call_target="tpu_custom_call" | custom-call | tf_op jit(solution)/shard_map/pallas_call | solution.py:636

commit v8 on v7

--- a/solution.py
+++ b/solution.py
@@ -12,7 +12,7 @@
 COMP, NPAR, COLS, PIPES, CELLS = 4, 2, 64, 8, 256
 LANES = 128
 Z_STEPS = (4, 3, 5, 2, 6, 1, 7)
-DIRECT = ((4, 0), (3, 0), (5, 1))
+DIRECT = ((4, 0), (3, 0), (5, 1), (6, 2))
 PE, PN, DD, CIN, COUT, WT = 0, 8, 16, 32, 48, 64
 N_COEF = 68
 J_W, J_ID, J_SPAN = 24, 28, 32

time: 18.5 us -> 18.5 us (level)
  no operation moved by 1% of the time
where the time goes in v8:
time: 18.5 us; the launch traced here: 18.3 us
  Pallas kernels  18.3 us (99%)
    pallas_call x1, Pallas kernels, on_device(): pl.pallas_call(kernel, out_shape=(pltpu.VMEM(directions.shape, F32), tile...  17.3 us
    pallas_call x1, Pallas kernels, on_device(): pl.pallas_call(write_kernel, out_shape=jax.ShapeDtypeStruct(directions.sh...  1.01 us

profile of v8, /device:TPU:32, one launch (start us, length us, event | category | flops | bytes accessed | tf_op | source)
XLA Modules:
  0.0 18.3 jit_solution(14580299193563907715)
XLA Ops:
  0.0 17.3 %shard_map.73 = (f32[2,64,8,256]{3,2,1,0:T(8,128)S(1)}, f32[2,8,128]{2,1,0:T(8,128)S(1)}) custom-call(f32[2,64,8,256]{3,2,1,0:T(8,128)} %dir_in.1, f32[4,4,8,256]{3,2,1,0:T(8,128)} %diag_in.1, f32[4,4,8,256]{3,2,1,0:T(8,128)} %left_in.1, f32[4,4,8,256]{3,2,1,0:T(8,128)} %right_in.1, f32[4,2,8,256]{3,2,1,0:T(8,128)} %par_in.1, f32[4,8,256]{2,1,0:T(8,128)} %wt_in.1, ...), custom_call_target="tpu_custom_call" | custom-call | tf_op jit(solution)/shard_map/pallas_call | solution.py:603
  17.3 1.0 %shard_map.74 = f32[2,64,8,256]{3,2,1,0:T(8,128)} custom-call(f32[2,64,8,256]{3,2,1,0:T(8,128)S(1)} %get-tuple-element.7.hess, f32[2,8,128]{2,1,0:T(8,128)S(1)} %get-tuple-element.8.last), custom_call_target="tpu_custom_call" | custom-call | tf_op jit(solution)/shard_map/pallas_call | solution.py:636
